TPU v7x, 1024 devices: a whole 4x4x32 slice. The times are simulated.
1024 devices in a mesh: member: 32 (over z), sx: 4 (over y_lo, core), sy: 8 (over x, y_hi).
Axes of the slice: x: 4, y: 4 (y_hi: 2, y_lo: 2; y = y_hi * 2 + y_lo), z: 32, core: 2. Of those that a mesh axis runs over, the one named last changes fastest.
Arguments:
- anomalies: bfloat16 [256, 3, 16, 128, 128], P('member', None, 'sx', 'sy'), may hold values from -6 to 6
- sigma: float32 [16, 128, 128], P('sx', 'sy'), may hold values from 0.5 to 2
- taper_x: float32 [16, 7], replicated, may hold values from 0.05 to 1
- taper_y: float32 [128, 7], replicated, may hold values from 0.05 to 1
- taper_z: float32 [128, 128], replicated, may hold values from -0.07 to 1.07
- innovation: float32 [4, 8, 2048], P('sx', 'sy'), may hold values from -6 to 6
- obs_inverse: float32 [4, 8, 2048], P('sx', 'sy'), may hold values from 0.25 to 4
- obs_index: int32 [4, 8, 2048], P('sx', 'sy'), may hold values from 0 to 8191
- obs_slot: int32 [4, 8, 2048], P('sx', 'sy'), may hold values from 0 to 2
Outputs:
- alpha_weights: float32 [256, 16, 128, 128], P('member', 'sx', 'sy')
- static_control: float32 [16, 128, 128], P('sx', 'sy')
- increment: float32 [3, 16, 128, 128], P(None, 'sx', 'sy')
All inputs are finite; a program needn't handle non-finite values.
Results may differ from a plain program's by a relative error of at most 0.001.
Values sent between devices are 32-bit elements; how exact they have to be, the bound alone decides.
No kernel may reach another device: no remote copies, remote signals or barrier semaphores. Data moves between devices by JAX's collectives and lax.ppermute only.
A program may use at most 32 MiB of HBM per device.

v0:
```python
import math

import jax
import jax.numpy as jnp
from jax import lax
from jax.sharding import PartitionSpec as P

HW = 3
ITERS = 2


STATIC_WEIGHT = 0.6


def padded_2(block, sides, width):
    for axis, dim in sides:
        count = lax.axis_size(axis)
        forward = [(i, i + 1) for i in range(count - 1)]
        backward = [(target, source) for source, target in forward]
        low = lax.ppermute(
            lax.slice_in_dim(block, block.shape[dim] - width, None, axis=dim), axis, forward
        )
        high = lax.ppermute(lax.slice_in_dim(block, 0, width, axis=dim), axis, backward)
        block = jnp.concatenate([low, block, high], axis=dim)
    return block


def body(anomalies, sigma, taper_x, taper_y, taper_z, innovation, obs_inverse, obs_index, obs_slot):
    local_members, slots, cells_x, cells_y, levels = anomalies.shape
    members = local_members * lax.axis_size("member")
    ens_weight = 0.8 / math.sqrt(members - 1)
    share = 1.0 / lax.axis_size("member")
    rows_x = lax.dynamic_slice_in_dim(taper_x, lax.axis_index("sx") * cells_x, cells_x, 0)
    rows_y = lax.dynamic_slice_in_dim(taper_y, lax.axis_index("sy") * cells_y, cells_y, 0)
    index_flat = obs_index.reshape(-1)
    slot_flat = obs_slot.reshape(-1)
    obs_weight = obs_inverse.reshape(-1)
    innov_flat = innovation.reshape(-1)

    def smooth_stack(stack):
        padded = padded_2(stack, (("sx", 1), ("sy", 2)), HW)
        along_x = jnp.zeros((stack.shape[0], cells_x, padded.shape[2], levels), jnp.float32)
        for offset in range(2 * HW + 1):
            along_x = (
                along_x
                + rows_x[:, offset][None, :, None, None] * padded[:, offset : offset + cells_x]
            )
        along_y = jnp.zeros(stack.shape, jnp.float32)
        for offset in range(2 * HW + 1):
            along_y = (
                along_y
                + rows_y[:, offset][None, None, :, None] * along_x[:, :, offset : offset + cells_y]
            )
        return jnp.einsum("bxyk,kl->bxyl", along_y, taper_z, precision=lax.Precision.HIGHEST)

    def spread(values):
        grid = jnp.zeros((slots, cells_x * cells_y * levels), jnp.float32)
        return grid.at[slot_flat, index_flat].add(values).reshape(slots, cells_x, cells_y, levels)

    def adjoint(values):
        grid = spread(values)
        ens_side = ens_weight * jnp.sum(anomalies.astype(jnp.float32) * grid[None], axis=1)
        static_side = STATIC_WEIGHT * sigma * jnp.sum(grid, axis=0)
        smoothed = smooth_stack(jnp.concatenate([ens_side, static_side[None]], axis=0))
        return (smoothed[:-1], smoothed[-1])

    def local_inner(left, right):
        return jnp.sum(left[0] * right[0]) + share * jnp.sum(left[1] * right[1])

    def inner(left, right):
        return lax.psum(local_inner(left, right), ("member", "sx", "sy"))

    def combine(first, scale, second):
        return jax.tree.map(lambda left, right: left + scale * right, first, second)

    rhs = adjoint(obs_weight * innov_flat)
    solution = jax.tree.map(jnp.zeros_like, rhs)
    residual = rhs
    empty_field = jnp.zeros((slots, cells_x, cells_y, levels), jnp.float32)
    increment = (empty_field, empty_field)
    direction = rhs
    norm_now = inner(residual, residual)
    for step in range(ITERS):
        forward_stack = jnp.concatenate([direction[0], direction[1][None]], axis=0)
        forward_smoothed = smooth_stack(forward_stack)
        ens_part = ens_weight * jnp.sum(
            anomalies.astype(jnp.float32) * forward_smoothed[:-1, None], axis=0
        )
        static = jnp.broadcast_to(
            (STATIC_WEIGHT * sigma * forward_smoothed[-1])[None], ens_part.shape
        )
        ens_sum = lax.psum(ens_part, "member")
        observed = (ens_sum + static).reshape(slots, -1)[slot_flat, index_flat]
        mapped = (ens_sum, static)
        grad_alpha, grad_static = adjoint(obs_weight * observed)
        image, mapped = ((direction[0] + grad_alpha, direction[1] + grad_static), mapped)
        step_size = norm_now / inner(direction, image)
        solution = combine(solution, step_size, direction)
        increment = combine(increment, step_size, mapped)
        if step + 1 < ITERS:
            residual = combine(residual, -step_size, image)
            norm_next = inner(residual, residual)
            direction = combine(residual, norm_next / norm_now, direction)
            norm_now = norm_next
    ens_total, static_total = increment
    return (solution[0], solution[1], ens_total + static_total)


def solution(mesh):
    return jax.shard_map(
        body,
        mesh=mesh,
        in_specs=(
            P("member", None, "sx", "sy", None),
            P("sx", "sy", None),
            P(),
            P(),
            P(),
            P("sx", "sy", None),
            P("sx", "sy", None),
            P("sx", "sy", None),
            P("sx", "sy", None),
        ),
        out_specs=(P("member", "sx", "sy", None), P("sx", "sy", None), P(None, "sx", "sy", None)),
        check_vma=False,
    )
```

profile of v0, /device:TPU:1, one launch (start us, length us, event | category | flops | bytes accessed | tf_op | source)
XLA Modules:
  0.0 1190.3 jit_solution(5411591140161625843)
XLA Ops:
  10.2 11.3 scatter_custom_fusion
  21.7 1.1 fusion
  22.9 4.6 collective-permute-start
  27.5 12.8 %collective-permute-start.1 = (f32[9,3,16,128]{3,2,1,0:T(8,128)S(1)}, f32[9,3,16,128]{3,2,1,0:T(8,128)S(1)}, u32[]{:S(2)}, u32[]{:S(2)}) collective-permute-start(f32[9,3,16,128]{3,2,1,0:T(8,128)S(1)} %get-tuple-element.28), channel_id=1, source_target_pairs={{8,0},{16,8},{24,16},{9,1},{17,9},{25,17},{10,2},{18,10},{26,18},{... | collective-permute-start | bytes 663560 | tf_op jit(solution)/shard_map/ppermute | solution.py:23
  41.4 1.3 collective-permute-start.2
  42.7 1.3 collective-permute-start.3
  44.0 4.6 collective-permute-done.2
  48.6 3.3 collective-permute-done.3
  53.1 1.9 collective-permute-start.4
  55.1 2.5 collective-permute-start.5
  57.9 8.1 collective-permute-done.5
  66.1 1.3 collective-permute-start.6
  67.4 1.3 collective-permute-start.7
  68.7 3.1 collective-permute-done.6
  71.8 3.4 collective-permute-done.7
  77.5 235.3 %all-reduce.4.cloned.1.call-done = f32[3,4,16,128]{3,2,1,0:T(8,128)} async-done(((f32[3,4,16,128]{3,2,1,0:T(8,128)}), f32[3,4,16,128]{3,2,1,0:T(8,128)}) %all-reduce.4.cloned.1.call-update) | async-done | bytes 98320 | tf_op jit(solution)/shard_map/psum | solution.py:92
  313.7 17.7 %gather_fusion = f32[2048]{0:T(1024)S(1)} fusion(f32[3,8192]{1,0:T(4,128)S(1)} %bitcast.127, s32[2048]{0:T(1024)S(1)} %bitcast.129), kind=kCustom, calls=%fused_computation | custom fusion | bytes 32768 | tf_op jit(solution)/shard_map/gather | solution.py:93
  331.5 11.3 scatter_custom_fusion.1
  343.1 25.8 %collective-permute-start.8 = (f32[9,3,16,128]{3,2,1,0:T(8,128)S(1)}, f32[9,3,16,128]{3,2,1,0:T(8,128)S(1)}, u32[]{:S(2)}, u32[]{:S(2)}) collective-permute-start(f32[9,3,16,128]{3,2,1,0:T(8,128)S(1)} %get-tuple-element.23), channel_id=1, source_target_pairs={{0,8},{8,16},{16,24},{1,9},{9,17},{17,25},{2,10},{10,18},{18,26},{... | collective-permute-start | bytes 663560 | tf_op jit(solution)/shard_map/ppermute | solution.py:20
  368.9 1.9 collective-permute-start.9
  370.8 0.9 collective-permute-done.8
  371.8 4.4 collective-permute-done.9
  376.2 4.4 collective-permute-start.10
  380.6 1.3 collective-permute-start.11
  381.9 3.1 collective-permute-done.10
  385.0 3.4 collective-permute-done.11
  393.3 152.4 %all-reduce = (f32[]{:T(128)}, f32[]{:T(128)}) all-reduce(f32[]{:T(128)S(6)} %add.315, f32[]{:T(128)S(6)} %add.343), channel_id=1, replica_groups=mesh['member'=32,'sx'=4,'sy'=8] {'member','sx','sy'}, use_global_device_ids=true, to_apply=%region_5.0 | all-reduce | flops 2 | bytes 16 | tf_op jit(solution)/shard_map/psum | solution.py:71
  549.7 152.3 %psum.45 = f32[]{:T(128)} all-reduce(f32[]{:T(128)S(6)} %add.346), channel_id=1, replica_groups=mesh['member'=32,'sx'=4,'sy'=8] {'member','sx','sy'}, use_global_device_ids=true, to_apply=%region_16.0 | all-reduce | flops 1 | bytes 8 | tf_op jit(solution)/shard_map/psum | solution.py:71
  703.4 3.2 collective-permute-start.12
  706.7 1.9 collective-permute-start.13
  708.6 0.9 collective-permute-done.12
  709.5 4.4 collective-permute-done.13
  714.0 4.3 collective-permute-start.14
  718.3 1.5 collective-permute-start.15
  719.7 4.9 collective-permute-done.14
  724.6 1.4 collective-permute-done.15
  728.0 220.4 %all-reduce.6.cloned.1.call-done = f32[3,4,16,128]{3,2,1,0:T(8,128)} async-done(((f32[3,4,16,128]{3,2,1,0:T(8,128)}), f32[3,4,16,128]{3,2,1,0:T(8,128)}) %all-reduce.6.cloned.1.call-update) | async-done | bytes 98320 | tf_op jit(solution)/shard_map/psum | solution.py:92
  949.3 17.7 %gather_fusion.1 = f32[2048]{0:T(1024)S(1)} fusion(f32[3,8192]{1,0:T(4,128)S(1)} %bitcast.128, s32[2048]{0:T(1024)S(1)} %bitcast.130), kind=kCustom, calls=%fused_computation.1 | custom fusion | bytes 32768 | tf_op jit(solution)/shard_map/gather | solution.py:93
  967.1 11.3 scatter_custom_fusion.2
  978.7 25.8 %collective-permute-start.16 = (f32[9,3,16,128]{3,2,1,0:T(8,128)S(1)}, f32[9,3,16,128]{3,2,1,0:T(8,128)S(1)}, u32[]{:S(2)}, u32[]{:S(2)}) collective-permute-start(f32[9,3,16,128]{3,2,1,0:T(8,128)S(1)} %get-tuple-element.19), channel_id=1, source_target_pairs={{0,8},{8,16},{16,24},{1,9},{9,17},{17,25},{2,10},{10,18},{18,26},{... | collective-permute-start | bytes 663560 | tf_op jit(solution)/shard_map/ppermute | solution.py:20
  1004.5 1.9 collective-permute-start.17
  1006.4 0.9 collective-permute-done.16
  1007.4 4.4 collective-permute-done.17
  1011.8 4.4 collective-permute-start.18
  1016.2 1.3 collective-permute-start.19
  1017.5 3.1 collective-permute-done.18
  1020.6 3.4 collective-permute-done.19
  1027.7 152.4 %psum.47 = f32[]{:T(128)} all-reduce(f32[]{:T(128)S(6)} %add.379), channel_id=1, replica_groups=mesh['member'=32,'sx'=4,'sy'=8] {'member','sx','sy'}, use_global_device_ids=true, to_apply=%region_24.0 | all-reduce | flops 1 | bytes 8 | tf_op jit(solution)/shard_map/psum | solution.py:71
  (96 shorter events, 20.9 us)
Async XLA Ops:
  7.2 45.3 %copy-start = (f32[128,128]{1,0:T(8,128)S(1)}, f32[128,128]{1,0:T(8,128)}, u32[]{:S(2)}) copy-start(f32[128,128]{1,0:T(8,128)} %param.13) | copy-start | bytes 196612
  7.2 15.6 %copy-start.2 = (f32[4,16,128]{2,1,0:T(8,128)S(1)}, f32[4,16,128]{2,1,0:T(8,128)}, u32[]{:S(2)}) copy-start(f32[4,16,128]{2,1,0:T(8,128)} %param.10) | copy-start | bytes 98308
  7.2 305.5 %all-reduce.4.cloned.1.call-start = ((), (), s32[]{:S(2)}) async-start(), calls=%async_computation | async-start | bytes 196608 | tf_op jit(solution)/shard_map/psum | solution.py:92
  21.6 18.6 %copy-start.6 = (f32[16,7]{0,1:T(8,128)S(1)}, f32[16,7]{0,1:T(8,128)}, u32[]{:S(2)}) copy-start(f32[16,7]{0,1:T(8,128)} %param.11) | copy-start | bytes 1348
  21.7 18.7 %copy-start.7 = (f32[128,7]{0,1:T(8,128)S(1)}, f32[128,7]{0,1:T(8,128)}, u32[]{:S(2)}) copy-start(f32[128,7]{0,1:T(8,128)} %param.12) | copy-start | bytes 10756
  22.9 17.6 %collective-permute-start = (f32[9,3,16,128]{3,2,1,0:T(8,128)S(1)}, f32[9,3,16,128]{3,2,1,0:T(8,128)S(1)}, u32[]{:S(2)}, u32[]{:S(2)}) collective-permute-start(f32[9,3,16,128]{3,2,1,0:T(8,128)S(1)} %get-tuple-element.27), channel_id=1, source_target_pairs={{0,8},{8,16},{16,24},{1,9},{9,17},{17,25},{2,10},{10,18},{18,26},{... | collective-permute-start | bytes 663560 | tf_op jit(solution)/shard_map/ppermute | solution.py:20
  27.5 13.9 %collective-permute-start.1 = (f32[9,3,16,128]{3,2,1,0:T(8,128)S(1)}, f32[9,3,16,128]{3,2,1,0:T(8,128)S(1)}, u32[]{:S(2)}, u32[]{:S(2)}) collective-permute-start(f32[9,3,16,128]{3,2,1,0:T(8,128)S(1)} %get-tuple-element.28), channel_id=1, source_target_pairs={{8,0},{16,8},{24,16},{9,1},{17,9},{25,17},{10,2},{18,10},{26,18},{... | collective-permute-start | bytes 663560 | tf_op jit(solution)/shard_map/ppermute | solution.py:23
  41.4 7.2 collective-permute-start.2
  42.7 9.2 collective-permute-start.3
  53.1 4.8 collective-permute-start.4
  55.1 10.9 collective-permute-start.5
  66.1 5.7 collective-permute-start.6
  67.4 7.8 collective-permute-start.7
  75.6 1.0 copy-start.1
  77.4 870.9 %all-reduce.6.cloned.1.call-start = ((), (), s32[]{:S(2)}) async-start(), calls=%async_computation.1 | async-start | bytes 196608 | tf_op jit(solution)/shard_map/psum | solution.py:92
  313.7 17.8 %copy-start.5 = (f32[1,1,2048]{2,1,0:T(1,128)S(1)}, f32[1,1,2048]{2,1,0:T(1,128)}, u32[]{:S(2)}) copy-start(f32[1,1,2048]{2,1,0:T(1,128)} %param.15) | copy-start | bytes 24580
  343.1 28.7 %collective-permute-start.8 = (f32[9,3,16,128]{3,2,1,0:T(8,128)S(1)}, f32[9,3,16,128]{3,2,1,0:T(8,128)S(1)}, u32[]{:S(2)}, u32[]{:S(2)}) collective-permute-start(f32[9,3,16,128]{3,2,1,0:T(8,128)S(1)} %get-tuple-element.23), channel_id=1, source_target_pairs={{0,8},{8,16},{16,24},{1,9},{9,17},{17,25},{2,10},{10,18},{18,26},{... | collective-permute-start | bytes 663560 | tf_op jit(solution)/shard_map/ppermute | solution.py:20
  368.9 7.3 collective-permute-start.9
  376.2 8.8 collective-permute-start.10
  380.6 7.8 collective-permute-start.11
  703.4 6.1 collective-permute-start.12
  706.7 7.3 collective-permute-start.13
  714.0 10.7 collective-permute-start.14
  718.3 7.8 collective-permute-start.15
  978.7 28.7 %collective-permute-start.16 = (f32[9,3,16,128]{3,2,1,0:T(8,128)S(1)}, f32[9,3,16,128]{3,2,1,0:T(8,128)S(1)}, u32[]{:S(2)}, u32[]{:S(2)}) collective-permute-start(f32[9,3,16,128]{3,2,1,0:T(8,128)S(1)} %get-tuple-element.19), channel_id=1, source_target_pairs={{0,8},{8,16},{16,24},{1,9},{9,17},{17,25},{2,10},{10,18},{18,26},{... | collective-permute-start | bytes 663560 | tf_op jit(solution)/shard_map/ppermute | solution.py:20
  1004.5 7.3 collective-permute-start.17
  1011.8 8.8 collective-permute-start.18
  1016.2 7.8 collective-permute-start.19
  1025.1 157.7 %copy-start.3 = (f32[3,4,16,128]{3,2,1,0:T(8,128)S(1)}, f32[3,4,16,128]{3,2,1,0:T(8,128)}, u32[]{:S(2)}) copy-start(f32[3,4,16,128]{3,2,1,0:T(8,128)} %all-reduce.4.cloned.1.call-done) | copy-start | bytes 294916
  1025.1 157.7 %copy-start.4 = (f32[3,4,16,128]{3,2,1,0:T(8,128)S(1)}, f32[3,4,16,128]{3,2,1,0:T(8,128)}, u32[]{:S(2)}) copy-start(f32[3,4,16,128]{3,2,1,0:T(8,128)} %all-reduce.6.cloned.1.call-done) | copy-start | bytes 294916
Sparse Core Ops, SparseCore 0:
  77.5 235.1 all-reduce.3
  728.1 220.2 all-reduce.5
where the time goes:
time: 1190 us
  waiting for transfers between devices  515 us (43%)
  blocking collectives  457 us (38%)
  starting transfers between devices  105 us (9%)
  other arithmetic  50.5 us (4%)
  local copies, waits for them, and re-layouts  36.3 us (3%)
  between operations  23.8 us (2%)
    psum x3, blocking collectives, inner(): return lax.psum(local_inner(left, right), ('member', 'sx', 'sy'))  457 us
    psum x2, waiting for transfers between devices, body(): ens_sum = lax.psum(ens_part, 'member')  456 us
    ppermute x10, starting transfers between devices, padded_2(): lax.ppermute(lax.slice_in_dim(block, block.shape[dim] - width, None, axis...  77 us
    ppermute x10, waiting for transfers between devices, padded_2(): lax.ppermute(lax.slice_in_dim(block, 0, width, axis=dim), axis, backward)  37 us
    gather x2, local copies, waits for them, and re-layouts, body(): observed = (ens_sum + static).reshape(slots, -1)[slot_flat, index_flat]  35.5 us
    unnamed x6, other arithmetic  35.3 us
    ppermute x10, starting transfers between devices, padded_2(): lax.ppermute(lax.slice_in_dim(block, 0, width, axis=dim), axis, backward)  27.7 us
  transfers between devices with their start and end apart: 22, of which 21 were waited for; matrix products, arithmetic and copies ran while one was open for 0% of the time, Pallas kernels for 0%

commit v1 on v0

v1 whole, which is shorter than its diff:
```python
import functools
import math

import jax
import jax.numpy as jnp
from jax import lax
from jax.experimental import pallas as pl
from jax.experimental.pallas import tpu as pltpu
from jax.sharding import PartitionSpec as P

HW = 3
STATIC_WEIGHT = 0.6
F32 = jnp.float32
BF16 = jnp.bfloat16
HIGH = lax.Precision.HIGH
HIGHEST = lax.Precision.HIGHEST


def halves(value):
    top = value.astype(BF16)
    return top, (value - top.astype(F32)).astype(BF16)


def one_hot(rows, index):
    return lax.broadcasted_iota(jnp.int32, (rows, index.shape[-1]), 0) == index


def spread_kernel(place_ref, weight_ref, grid_ref):
    cells, levels = grid_ref.shape
    at_cell = one_hot(cells, place_ref[0:1, :]).astype(BF16)
    at_level = one_hot(levels, place_ref[1:2, :])
    top, low = halves(jnp.where(at_level, weight_ref[...], 0.0))
    contract = (((1,), (1,)), ((), ()))
    grid_ref[...] = lax.dot_general(
        at_cell, top, contract, preferred_element_type=F32
    ) + lax.dot_general(at_cell, low, contract, preferred_element_type=F32)


def sample_kernel(place_ref, field_ref, value_ref):
    fields, cells, levels = field_ref.shape
    at_cell = one_hot(cells, place_ref[0:1, :]).astype(BF16)
    at_level = one_hot(levels, place_ref[1:2, :])
    contract = (((0,), (0,)), ((), ()))
    for i in range(fields):
        top, low = halves(field_ref[i])
        columns = lax.dot_general(
            top, at_cell, contract, preferred_element_type=F32
        ) + lax.dot_general(low, at_cell, contract, preferred_element_type=F32)
        value_ref[i : i + 1, :] = jnp.sum(jnp.where(at_level, columns, 0.0), axis=0, keepdims=True)


def groups(size, width, stride):
    seen, out = set(), []
    for first in range(size):
        if first not in seen:
            members = [first + stride * k for k in range(width)]
            seen.update(members)
            out.append(members)
    return out


def exchange(blocks, axis, index_groups=None):
    return lax.all_to_all(blocks, axis, 0, 0, axis_index_groups=index_groups, tiled=True)


def gathered(block, width, axis, index_groups=None):
    return exchange(jnp.broadcast_to(block[None], (width,) + block.shape), axis, index_groups)


def neighbours(low_side, high_side, axis):
    count = lax.axis_size(axis)
    up = [(i, i + 1) for i in range(count - 1)]
    down = [(j, i) for i, j in up]
    return lax.ppermute(high_side, axis, up), lax.ppermute(low_side, axis, down)


def taps(field, table, dim, count):
    total = None
    for offset in range(2 * HW + 1):
        shape = [1] * field.ndim
        shape[dim] = count
        term = table[:, offset].reshape(shape) * lax.slice_in_dim(field, offset, offset + count, axis=dim)
        total = term if total is None else total + term
    return total


def flipped(table):
    rows = table.shape[0]
    padded = jnp.pad(table, ((HW, HW), (0, 0)))
    return jnp.stack([padded[o : o + rows, 2 * HW - o] for o in range(2 * HW + 1)], axis=1)


def window(table, axis, count, rim):
    padded = jnp.pad(table, ((rim, rim), (0, 0)))
    return lax.dynamic_slice_in_dim(padded, lax.axis_index(axis) * count, count + 2 * rim, 0)


def body(anomalies, sigma, taper_x, taper_y, taper_z, innovation, obs_inverse, obs_index, obs_slot):
    local_members, slots, cells_x, cells_y, levels = anomalies.shape
    member_devices = lax.axis_size("member")
    ens_weight = 0.8 / math.sqrt(local_members * member_devices - 1)
    share = 1.0 / member_devices
    cells = cells_x * cells_y
    count = obs_index.shape[-1]
    rows = count // levels

    near = 8 if member_devices % 8 == 0 else 1
    far = member_devices // near
    near_groups = groups(member_devices, near, 1)
    far_groups = groups(member_devices, far, near)
    close = 4 if member_devices % 4 == 0 else 1
    wide = member_devices // close
    close_groups = groups(member_devices, close, 1)
    wide_groups = groups(member_devices, wide, close)

    index_flat = obs_index.reshape(1, -1)
    place = jnp.concatenate(
        [obs_slot.reshape(1, -1) * cells + index_flat // levels, index_flat % levels], axis=0
    )
    obs_weight = obs_inverse.reshape(1, -1)
    first_weight = obs_weight * innovation.reshape(1, -1)

    x_rows = window(taper_x, "sx", cells_x, 0)
    x_flip = window(flipped(taper_x), "sx", cells_x, 0)
    y_rows_wide = window(taper_y, "sy", cells_y, HW)
    y_rows = y_rows_wide[HW : HW + cells_y]
    y_flip = window(flipped(taper_y), "sy", cells_y, 0)
    x_pair = jnp.stack([x_rows, x_flip])
    y_pair = jnp.stack([y_rows, y_flip])
    z_pair = jnp.stack([taper_z, taper_z.T])

    def spread(weights):
        return pl.pallas_call(
            spread_kernel,
            out_shape=jax.ShapeDtypeStruct((slots * cells, levels), F32),
            compiler_params=pltpu.CompilerParams(vmem_limit_bytes=32 * 2**20),
        )(place, weights).reshape(slots, cells_x, cells_y, levels)

    def sample(fields):
        return pl.pallas_call(
            sample_kernel,
            out_shape=jax.ShapeDtypeStruct((fields.shape[0], count), F32),
            compiler_params=pltpu.CompilerParams(vmem_limit_bytes=32 * 2**20),
        )(place, fields.reshape(fields.shape[0], slots * cells, levels))

    def apply(weights):
        grid = spread(weights)
        ens_side = ens_weight * jnp.sum(anomalies.astype(F32) * grid[None], axis=1)
        static_side = STATIC_WEIGHT * sigma * jnp.sum(grid, axis=0)
        stack = jnp.concatenate([ens_side, static_side[None]], axis=0)
        left, right = neighbours(stack[:, :, : 2 * HW], stack[:, :, cells_y - 2 * HW :], "sy")
        stack = jnp.concatenate([left, stack, right], axis=2)
        wide_y = cells_y + 2 * HW
        stack = taps(stack, y_rows_wide, 2, wide_y)
        above, below = neighbours(stack[:, :HW], stack[:, cells_x - HW :], "sx")
        stack = taps(jnp.concatenate([above, stack, below], axis=1), x_rows, 1, cells_x)
        stack = jnp.einsum("bxyk,kl->bxyl", stack, taper_z, precision=HIGH)
        control = stack[:, :, HW : HW + cells_y]
        above, below = neighbours(stack[:, :HW], stack[:, cells_x - HW :], "sx")
        stack = jnp.concatenate([above, stack, below], axis=1)
        fields = []
        for which in range(2):
            out = taps(stack, x_pair[which], 1, cells_x)
            out = taps(out, y_pair[which], 2, cells_y)
            out = jnp.einsum("bxyk,kl->bxyl", out, z_pair[which], precision=HIGH)
            ens_part = ens_weight * jnp.sum(anomalies.astype(F32) * out[:-1, None], axis=0)
            fields.append(ens_part + (share * STATIC_WEIGHT) * (sigma * out[-1])[None])
        sampled = sample(jnp.stack(fields)).reshape(2, rows, levels)
        return control, fields[0], sampled

    control0, field0, sampled0 = apply(first_weight)
    part = jnp.sum(gathered(sampled0[0], close, "member", close_groups), axis=0)
    seen0 = jnp.sum(gathered(part, wide, "member", wide_groups), axis=0)
    obs_rows = obs_weight.reshape(rows, levels)
    weight1 = obs_rows * seen0
    control1, field1, sampled1 = apply(weight1.reshape(1, -1))

    flat = jnp.concatenate(
        [
            block.reshape(near, -1, levels)
            for block in (sampled0[1], sampled1[0], sampled1[1], field0, field1)
        ],
        axis=1,
    )
    chunk = jnp.sum(exchange(flat, "member", near_groups), axis=0)
    chunk = jnp.sum(gathered(chunk, far, "member", far_groups), axis=0)
    total = gathered(chunk, near, "member", near_groups)
    obs_chunk = rows // near
    seen = total[:, : 3 * obs_chunk].reshape(near, 3, obs_chunk, levels)
    flip0, seen1, flip1 = (seen[:, i].reshape(rows, levels) for i in range(3))
    fields = total[:, 3 * obs_chunk :].reshape(near, 2, -1, levels)
    total0, total1 = (fields[:, i].reshape(slots, cells_x, cells_y, levels) for i in range(2))

    weight0 = first_weight.reshape(rows, levels)
    weight2 = obs_rows * seen1
    products = jnp.stack(
        [
            jnp.sum(a * b, axis=0)
            for a, b in (
                (weight0, flip0),
                (weight1, flip0),
                (weight1, flip1),
                (weight2, flip0),
                (weight2, flip1),
            )
        ]
    )
    regions = lax.axis_size("sx") * lax.axis_size("sy")
    products = jnp.sum(gathered(products, regions, ("sx", "sy")), axis=(0, 2))
    p00, p01, p11, p02, p12 = (products[i] for i in range(5))

    step0 = p00 / (p00 + p01)
    keep = 1.0 - step0
    next_norm = keep * (keep * p00 - 2.0 * step0 * p01) + step0 * step0 * p11
    beta = next_norm / p00
    lead = keep + beta
    own = lead * (lead * p00 - 2.0 * step0 * p01) + step0 * step0 * p11
    cross = lead * (lead * p01 - step0 * p02) - step0 * (lead * p11 - step0 * p12)
    step1 = next_norm / (own + cross)
    mix0 = step0 + step1 * lead
    mix1 = -step1 * step0
    control = mix0 * control0 + mix1 * control1
    increment = mix0 * total0 + mix1 * total1
    return control[:-1], control[-1], increment


def solution(mesh):
    return jax.shard_map(
        body,
        mesh=mesh,
        in_specs=(
            P("member", None, "sx", "sy", None),
            P("sx", "sy", None),
            P(),
            P(),
            P(),
            P("sx", "sy", None),
            P("sx", "sy", None),
            P("sx", "sy", None),
            P("sx", "sy", None),
        ),
        out_specs=(P("member", "sx", "sy", None), P("sx", "sy", None), P(None, "sx", "sy", None)),
        check_vma=False,
    )
```

time: 1190 us -> 239 us (0.20)
  waiting for transfers between devices: 515 us -> 39.3 us
  blocking collectives: 457 us -> 116 us
  starting transfers between devices: 105 us -> 53.4 us
  other arithmetic: 50.5 us -> 5.67 us
  local copies, waits for them, and re-layouts: 36.3 us -> 8.55 us
  between operations: 23.8 us -> 8.83 us
    psum x3 -> x0, blocking collectives: 457 us -> none  [inner(): return lax.psum(local_inner(left, right), ('member', 'sx', 'sy'))]
    psum x2 -> x0, waiting for transfers between devices: 456 us -> none  [body(): ens_sum = lax.psum(ens_part, 'member')]
    all_to_all x0 -> x5, blocking collectives: none -> 116 us  [exchange(): lax.all_to_all(blocks, axis, 0, 0, axis_index_groups=index_groups, tiled=...]
    ppermute x20 -> x12, starting transfers between devices: 105 us -> 42.6 us  [the longest x6 22.6 us: neighbours(): lax.ppermute(high_side, axis, up)]
    gather x2 -> x0, local copies, waits for them, and re-layouts: 35.5 us -> none  [body(): observed = (ens_sum + static).reshape(slots, -1)[slot_flat, index_flat]]
    unnamed x6 -> x0, other arithmetic: 35.3 us -> none
    ppermute x20 -> x12, waiting for transfers between devices: 59 us -> 31.6 us  [the longest x6 24.1 us: neighbours(): lax.ppermute(low_side, axis, down)]
  transfers between devices with their start and end apart: 22 -> 13, of which waited for: 21 -> 11; matrix products, arithmetic and copies ran while one was open for 0% -> 0% of each run, Pallas kernels for 0% -> 0%
where the time goes in v1:
time: 239 us; the launch traced here: 238 us
  blocking collectives  116 us (49%)
  starting transfers between devices  53.4 us (22%)
  waiting for transfers between devices  39.3 us (16%)
  between operations  8.83 us (4%)
  local copies, waits for them, and re-layouts  8.55 us (4%)
  other arithmetic  5.67 us (2%)
  matrix products  3.15 us (1%)
  Pallas kernels  2.89 us (1%)
    all_to_all x5, blocking collectives, exchange(): lax.all_to_all(blocks, axis, 0, 0, axis_index_groups=index_groups, tiled=...  116 us
    ppermute x6, waiting for transfers between devices, neighbours(): lax.ppermute(low_side, axis, down)  24.1 us
    ppermute x6, starting transfers between devices, neighbours(): lax.ppermute(high_side, axis, up)  22.6 us
    ppermute x6, starting transfers between devices, neighbours(): lax.ppermute(low_side, axis, down)  20 us
    all_to_all x1, starting transfers between devices, exchange(): lax.all_to_all(blocks, axis, 0, 0, axis_index_groups=index_groups, tiled=...  10.8 us
    all_to_all x1, waiting for transfers between devices, exchange(): lax.all_to_all(blocks, axis, 0, 0, axis_index_groups=index_groups, tiled=...  7.71 us
    ppermute x6, waiting for transfers between devices, neighbours(): lax.ppermute(high_side, axis, up)  7.56 us
  transfers between devices with their start and end apart: 13, of which 11 were waited for; matrix products, arithmetic and copies ran while one was open for 0% of the time, Pallas kernels for 0%

profile of v1, /device:TPU:1, one launch (start us, length us, event | category | flops | bytes accessed | tf_op | source)
XLA Modules:
  0.0 237.6 jit_solution(1266109302959808076)
XLA Ops:
  0.6 0.8 bitcast_add_fusion
  1.5 0.7 copy-done.5
  2.2 0.6 shard_map.112
  2.8 1.1 fusion
  3.9 0.7 copy-done.4
  4.7 5.7 %collective-permute-start = (f32[9,4,6,128]{3,2,1,0:T(8,128)S(1)}, f32[9,4,6,128]{3,2,1,0:T(8,128)S(1)}, u32[]{:S(2)}, u32[]{:S(2)}) collective-permute-start(f32[9,4,6,128]{3,2,1,0:T(8,128)S(1)} %get-tuple-element.22), channel_id=1, source_target_pairs={{0,1},{1,2},{2,3},{3,4},{4,5},{5,6},{6,7},{8,9},{9,10},{10,11},{11... | collective-permute-start | bytes 331784 | tf_op jit(solution)/shard_map/ppermute | solution.py:74
  10.4 1.3 collective-permute-start.1
  11.7 0.7 copy-done.7
  12.6 0.6 copy-done.8
  13.4 4.4 %collective-permute-done.1 = f32[9,4,6,128]{3,2,1,0:T(8,128)S(1)} collective-permute-done((f32[9,4,6,128]{3,2,1,0:T(8,128)S(1)}, f32[9,4,6,128]{3,2,1,0:T(8,128)S(1)}, u32[]{:S(2)}, u32[]{:S(2)}) %collective-permute-start.1) | collective-permute-done | bytes 110624 | tf_op jit(solution)/shard_map/ppermute | solution.py:74
  18.3 4.5 %collective-permute-start.2 = (f32[9,3,22,128]{3,2,1,0:T(8,128)S(1)}, f32[9,3,22,128]{3,2,1,0:T(8,128)S(1)}, u32[]{:S(2)}, u32[]{:S(2)}) collective-permute-start(f32[9,3,22,128]{3,2,1,0:T(8,128)S(1)} %get-tuple-element.18), channel_id=1, source_target_pairs={{0,8},{8,16},{16,24},{1,9},{9,17},{17,25},{2,10},{10,18},{18,26},{... | collective-permute-start | bytes 912392 | tf_op jit(solution)/shard_map/ppermute | solution.py:74
  22.8 10.7 %collective-permute-start.3 = (f32[9,3,22,128]{3,2,1,0:T(8,128)S(1)}, f32[9,3,22,128]{3,2,1,0:T(8,128)S(1)}, u32[]{:S(2)}, u32[]{:S(2)}) collective-permute-start(f32[9,3,22,128]{3,2,1,0:T(8,128)S(1)} %get-tuple-element.19), channel_id=1, source_target_pairs={{8,0},{16,8},{24,16},{9,1},{17,9},{25,17},{10,2},{18,10},{26,18},{... | collective-permute-start | bytes 912392 | tf_op jit(solution)/shard_map/ppermute | solution.py:74
  33.5 1.2 collective-permute-done.3
  34.7 0.5 fusion.37
  35.3 1.9 collective-permute-start.4
  37.3 2.4 %collective-permute-start.5 = (f32[9,3,22,128]{3,2,1,0:T(8,128)S(1)}, f32[9,3,22,128]{3,2,1,0:T(8,128)S(1)}, u32[]{:S(2)}, u32[]{:S(2)}) collective-permute-start(f32[9,3,22,128]{3,2,1,0:T(8,128)S(1)} %get-tuple-element.16), channel_id=1, source_target_pairs={{8,0},{16,8},{24,16},{9,1},{17,9},{25,17},{10,2},{18,10},{26,18},{... | collective-permute-start | bytes 912392 | tf_op jit(solution)/shard_map/ppermute | solution.py:74
  39.8 1.5 collective-permute-done.4
  41.3 4.4 %collective-permute-done.5 = f32[9,3,22,128]{3,2,1,0:T(8,128)S(1)} collective-permute-done((f32[9,3,22,128]{3,2,1,0:T(8,128)S(1)}, f32[9,3,22,128]{3,2,1,0:T(8,128)S(1)}, u32[]{:S(2)}, u32[]{:S(2)}) %collective-permute-start.5) | collective-permute-done | bytes 304160 | tf_op jit(solution)/shard_map/ppermute | solution.py:74
  47.4 0.9 copy-done.1
  48.6 0.9 shard_map.113
  49.5 6.9 %all_to_all.30 = f32[4,16,128]{2,1,0:T(8,128)S(1)} all-to-all(f32[4,16,128]{2,1,0:T(8,128)S(1)} %broadcast_in_dim.18), channel_id=1, replica_groups={{0,32,64,96},{128,160,192,224},{256,288,320,352},{384,416,448,480},{512..., dimensions={0} | all-to-all | bytes 65536 | tf_op jit(solution)/shard_map/all_to_all | solution.py:63
  56.4 47.1 %all_to_all.31 = f32[8,16,128]{2,1,0:T(8,128)S(1)} all-to-all(f32[8,16,128]{2,1,0:T(8,128)S(1)} %broadcast_in_dim.19), channel_id=1, replica_groups={{0,128,256,384,512,640,768,896},{32,160,288,416,544,672,800,928},{64,19..., dimensions={0} | all-to-all | bytes 131072 | tf_op jit(solution)/shard_map/all_to_all | solution.py:63
  103.6 0.6 shard_map.114
  104.3 5.3 %collective-permute-start.6 = (f32[9,4,6,128]{3,2,1,0:T(8,128)S(1)}, f32[9,4,6,128]{3,2,1,0:T(8,128)S(1)}, u32[]{:S(2)}, u32[]{:S(2)}) collective-permute-start(f32[9,4,6,128]{3,2,1,0:T(8,128)S(1)} %get-tuple-element.20), channel_id=1, source_target_pairs={{0,1},{1,2},{2,3},{3,4},{4,5},{5,6},{6,7},{8,9},{9,10},{10,11},{11... | collective-permute-start | bytes 331784 | tf_op jit(solution)/shard_map/ppermute | solution.py:74
  109.6 1.3 collective-permute-start.7
  110.9 2.3 collective-permute-done.6
  113.2 5.3 %collective-permute-done.7 = f32[9,4,6,128]{3,2,1,0:T(8,128)S(1)} collective-permute-done((f32[9,4,6,128]{3,2,1,0:T(8,128)S(1)}, f32[9,4,6,128]{3,2,1,0:T(8,128)S(1)}, u32[]{:S(2)}, u32[]{:S(2)}) %collective-permute-start.7) | collective-permute-done | bytes 110624 | tf_op jit(solution)/shard_map/ppermute | solution.py:74
  119.1 3.3 %collective-permute-start.8 = (f32[9,3,22,128]{3,2,1,0:T(8,128)S(1)}, f32[9,3,22,128]{3,2,1,0:T(8,128)S(1)}, u32[]{:S(2)}, u32[]{:S(2)}) collective-permute-start(f32[9,3,22,128]{3,2,1,0:T(8,128)S(1)} %get-tuple-element.14), channel_id=1, source_target_pairs={{0,8},{8,16},{16,24},{1,9},{9,17},{17,25},{2,10},{10,18},{18,26},{... | collective-permute-start | bytes 912392 | tf_op jit(solution)/shard_map/ppermute | solution.py:74
  122.5 1.9 collective-permute-start.9
  124.4 2.1 collective-permute-done.8
  126.5 4.4 %collective-permute-done.9 = f32[9,3,22,128]{3,2,1,0:T(8,128)S(1)} collective-permute-done((f32[9,3,22,128]{3,2,1,0:T(8,128)S(1)}, f32[9,3,22,128]{3,2,1,0:T(8,128)S(1)}, u32[]{:S(2)}, u32[]{:S(2)}) %collective-permute-start.9) | collective-permute-done | bytes 304160 | tf_op jit(solution)/shard_map/ppermute | solution.py:74
  130.9 0.6 fusion.14
  131.5 1.9 collective-permute-start.10
  133.5 2.4 %collective-permute-start.11 = (f32[9,3,22,128]{3,2,1,0:T(8,128)S(1)}, f32[9,3,22,128]{3,2,1,0:T(8,128)S(1)}, u32[]{:S(2)}, u32[]{:S(2)}) collective-permute-start(f32[9,3,22,128]{3,2,1,0:T(8,128)S(1)} %get-tuple-element.12), channel_id=1, source_target_pairs={{8,0},{16,8},{24,16},{9,1},{17,9},{25,17},{10,2},{18,10},{26,18},{... | collective-permute-start | bytes 912392 | tf_op jit(solution)/shard_map/ppermute | solution.py:74
  135.9 1.6 collective-permute-done.10
  137.5 4.4 %collective-permute-done.11 = f32[9,3,22,128]{3,2,1,0:T(8,128)S(1)} collective-permute-done((f32[9,3,22,128]{3,2,1,0:T(8,128)S(1)}, f32[9,3,22,128]{3,2,1,0:T(8,128)S(1)}, u32[]{:S(2)}, u32[]{:S(2)}) %collective-permute-start.11) | collective-permute-done | bytes 304160 | tf_op jit(solution)/shard_map/ppermute | solution.py:74
  143.6 0.9 slice-done.1
  144.7 0.9 shard_map.115
  146.0 14.8 %all_to_all.32 = f32[8,54,128]{2,1,0:T(8,128)S(1)} all-to-all(f32[8,54,128]{2,1,0:T(8,128)S(1)} %concatenate.93), channel_id=1, replica_groups={{0,32,64,96,128,160,192,224},{256,288,320,352,384,416,448,480},{512,544..., dimensions={0} | all-to-all | bytes 442368 | tf_op jit(solution)/shard_map/all_to_all | solution.py:63
  160.8 28.1 %all_to_all.33 = f32[4,54,128]{2,1,0:T(8,128)S(1)} all-to-all(f32[4,54,128]{2,1,0:T(8,128)S(1)} %broadcast_in_dim.21), channel_id=1, replica_groups={{0,256,512,768},{32,288,544,800},{64,320,576,832},{96,352,608,864},{128..., dimensions={0} | all-to-all | bytes 221184 | tf_op jit(solution)/shard_map/all_to_all | solution.py:63
  189.0 18.9 %all_to_all.34 = f32[8,54,128]{2,1,0:T(8,128)S(1)} all-to-all(f32[8,54,128]{2,1,0:T(8,128)S(1)} %broadcast_in_dim.22), channel_id=1, replica_groups={{0,32,64,96,128,160,192,224},{256,288,320,352,384,416,448,480},{512,544..., dimensions={0} | all-to-all | bytes 442368 | tf_op jit(solution)/shard_map/all_to_all | solution.py:63
  208.0 0.7 broadcast_in_dim.23
  208.6 10.8 %all-to-all-start.5 = ((f32[32,5,128]{2,1,0:T(8,128)}), f32[32,5,128]{2,1,0:T(8,128)S(1)}, u32[]{:S(2)}, u32[]{:S(2)}) async-start(f32[32,5,128]{2,1,0:T(8,128)} %broadcast_in_dim.23), calls=%async_computation.5 | async-start | bytes 262144 | tf_op jit(solution)/shard_map/all_to_all | solution.py:63
  219.4 7.7 %all-to-all-done.5 = f32[32,5,128]{2,1,0:T(8,128)S(1)} async-done(((f32[32,5,128]{2,1,0:T(8,128)}), f32[32,5,128]{2,1,0:T(8,128)S(1)}, u32[]{:S(2)}, u32[]{:S(2)}) %all-to-all-start.5) | async-done | bytes 81952 | tf_op jit(solution)/shard_map/all_to_all | solution.py:63
  227.3 0.7 fusion.199
  235.6 0.7 slice.811
  236.3 0.6 slice_bitcast_fusion
  236.9 0.7 fusion.175
  (89 shorter events, 6.5 us)
Async XLA Ops:
  0.6 34.1 %copy-start = (f32[128,128]{1,0:T(8,128)S(1)}, f32[128,128]{1,0:T(8,128)}, u32[]{:S(2)}) copy-start(f32[128,128]{1,0:T(8,128)} %param.13) | copy-start | bytes 196612
  1.5 0.7 copy-start.5
  1.5 0.7 copy-start.6
  3.9 0.8 copy-start.4
  4.7 8.7 %collective-permute-start = (f32[9,4,6,128]{3,2,1,0:T(8,128)S(1)}, f32[9,4,6,128]{3,2,1,0:T(8,128)S(1)}, u32[]{:S(2)}, u32[]{:S(2)}) collective-permute-start(f32[9,4,6,128]{3,2,1,0:T(8,128)S(1)} %get-tuple-element.22), channel_id=1, source_target_pairs={{0,1},{1,2},{2,3},{3,4},{4,5},{5,6},{6,7},{8,9},{9,10},{10,11},{11... | collective-permute-start | bytes 331784 | tf_op jit(solution)/shard_map/ppermute | solution.py:74
  10.4 7.4 %collective-permute-start.1 = (f32[9,4,6,128]{3,2,1,0:T(8,128)S(1)}, f32[9,4,6,128]{3,2,1,0:T(8,128)S(1)}, u32[]{:S(2)}, u32[]{:S(2)}) collective-permute-start(f32[9,4,6,128]{3,2,1,0:T(8,128)S(1)} %get-tuple-element.23), channel_id=1, source_target_pairs={{1,0},{2,1},{3,2},{4,3},{5,4},{6,5},{7,6},{9,8},{10,9},{11,10},{12... | collective-permute-start | bytes 331784 | tf_op jit(solution)/shard_map/ppermute | solution.py:74
  11.7 0.7 copy-start.7
  12.5 0.7 copy-start.8
  18.3 15.2 %collective-permute-start.2 = (f32[9,3,22,128]{3,2,1,0:T(8,128)S(1)}, f32[9,3,22,128]{3,2,1,0:T(8,128)S(1)}, u32[]{:S(2)}, u32[]{:S(2)}) collective-permute-start(f32[9,3,22,128]{3,2,1,0:T(8,128)S(1)} %get-tuple-element.18), channel_id=1, source_target_pairs={{0,8},{8,16},{16,24},{1,9},{9,17},{17,25},{2,10},{10,18},{18,26},{... | collective-permute-start | bytes 912392 | tf_op jit(solution)/shard_map/ppermute | solution.py:74
  22.8 11.9 %collective-permute-start.3 = (f32[9,3,22,128]{3,2,1,0:T(8,128)S(1)}, f32[9,3,22,128]{3,2,1,0:T(8,128)S(1)}, u32[]{:S(2)}, u32[]{:S(2)}) collective-permute-start(f32[9,3,22,128]{3,2,1,0:T(8,128)S(1)} %get-tuple-element.19), channel_id=1, source_target_pairs={{8,0},{16,8},{24,16},{9,1},{17,9},{25,17},{10,2},{18,10},{26,18},{... | collective-permute-start | bytes 912392 | tf_op jit(solution)/shard_map/ppermute | solution.py:74
  35.3 6.0 %collective-permute-start.4 = (f32[9,3,22,128]{3,2,1,0:T(8,128)S(1)}, f32[9,3,22,128]{3,2,1,0:T(8,128)S(1)}, u32[]{:S(2)}, u32[]{:S(2)}) collective-permute-start(f32[9,3,22,128]{3,2,1,0:T(8,128)S(1)} %get-tuple-element.17), channel_id=1, source_target_pairs={{0,8},{8,16},{16,24},{1,9},{9,17},{17,25},{2,10},{10,18},{18,26},{... | collective-permute-start | bytes 912392 | tf_op jit(solution)/shard_map/ppermute | solution.py:74
  37.3 8.4 %collective-permute-start.5 = (f32[9,3,22,128]{3,2,1,0:T(8,128)S(1)}, f32[9,3,22,128]{3,2,1,0:T(8,128)S(1)}, u32[]{:S(2)}, u32[]{:S(2)}) collective-permute-start(f32[9,3,22,128]{3,2,1,0:T(8,128)S(1)} %get-tuple-element.16), channel_id=1, source_target_pairs={{8,0},{16,8},{24,16},{9,1},{17,9},{25,17},{10,2},{18,10},{26,18},{... | collective-permute-start | bytes 912392 | tf_op jit(solution)/shard_map/ppermute | solution.py:74
  46.5 0.8 copy-start.2
  47.3 1.0 copy-start.1
  47.4 1.0 slice-start
  104.3 8.9 %collective-permute-start.6 = (f32[9,4,6,128]{3,2,1,0:T(8,128)S(1)}, f32[9,4,6,128]{3,2,1,0:T(8,128)S(1)}, u32[]{:S(2)}, u32[]{:S(2)}) collective-permute-start(f32[9,4,6,128]{3,2,1,0:T(8,128)S(1)} %get-tuple-element.20), channel_id=1, source_target_pairs={{0,1},{1,2},{2,3},{3,4},{4,5},{5,6},{6,7},{8,9},{9,10},{10,11},{11... | collective-permute-start | bytes 331784 | tf_op jit(solution)/shard_map/ppermute | solution.py:74
  109.6 9.0 %collective-permute-start.7 = (f32[9,4,6,128]{3,2,1,0:T(8,128)S(1)}, f32[9,4,6,128]{3,2,1,0:T(8,128)S(1)}, u32[]{:S(2)}, u32[]{:S(2)}) collective-permute-start(f32[9,4,6,128]{3,2,1,0:T(8,128)S(1)} %get-tuple-element.21), channel_id=1, source_target_pairs={{1,0},{2,1},{3,2},{4,3},{5,4},{6,5},{7,6},{9,8},{10,9},{11,10},{12... | collective-permute-start | bytes 331784 | tf_op jit(solution)/shard_map/ppermute | solution.py:74
  119.1 7.4 %collective-permute-start.8 = (f32[9,3,22,128]{3,2,1,0:T(8,128)S(1)}, f32[9,3,22,128]{3,2,1,0:T(8,128)S(1)}, u32[]{:S(2)}, u32[]{:S(2)}) collective-permute-start(f32[9,3,22,128]{3,2,1,0:T(8,128)S(1)} %get-tuple-element.14), channel_id=1, source_target_pairs={{0,8},{8,16},{16,24},{1,9},{9,17},{17,25},{2,10},{10,18},{18,26},{... | collective-permute-start | bytes 912392 | tf_op jit(solution)/shard_map/ppermute | solution.py:74
  122.5 8.4 %collective-permute-start.9 = (f32[9,3,22,128]{3,2,1,0:T(8,128)S(1)}, f32[9,3,22,128]{3,2,1,0:T(8,128)S(1)}, u32[]{:S(2)}, u32[]{:S(2)}) collective-permute-start(f32[9,3,22,128]{3,2,1,0:T(8,128)S(1)} %get-tuple-element.15), channel_id=1, source_target_pairs={{8,0},{16,8},{24,16},{9,1},{17,9},{25,17},{10,2},{18,10},{26,18},{... | collective-permute-start | bytes 912392 | tf_op jit(solution)/shard_map/ppermute | solution.py:74
  131.5 6.0 %collective-permute-start.10 = (f32[9,3,22,128]{3,2,1,0:T(8,128)S(1)}, f32[9,3,22,128]{3,2,1,0:T(8,128)S(1)}, u32[]{:S(2)}, u32[]{:S(2)}) collective-permute-start(f32[9,3,22,128]{3,2,1,0:T(8,128)S(1)} %get-tuple-element.13), channel_id=1, source_target_pairs={{0,8},{8,16},{16,24},{1,9},{9,17},{17,25},{2,10},{10,18},{18,26},{... | collective-permute-start | bytes 912392 | tf_op jit(solution)/shard_map/ppermute | solution.py:74
  133.5 8.4 %collective-permute-start.11 = (f32[9,3,22,128]{3,2,1,0:T(8,128)S(1)}, f32[9,3,22,128]{3,2,1,0:T(8,128)S(1)}, u32[]{:S(2)}, u32[]{:S(2)}) collective-permute-start(f32[9,3,22,128]{3,2,1,0:T(8,128)S(1)} %get-tuple-element.12), channel_id=1, source_target_pairs={{8,0},{16,8},{24,16},{9,1},{17,9},{25,17},{10,2},{18,10},{26,18},{... | collective-permute-start | bytes 912392 | tf_op jit(solution)/shard_map/ppermute | solution.py:74
  142.7 0.8 copy-start.3
  143.6 1.0 slice-start.1
  208.6 18.5 %all-to-all-start.5 = ((f32[32,5,128]{2,1,0:T(8,128)}), f32[32,5,128]{2,1,0:T(8,128)S(1)}, u32[]{:S(2)}, u32[]{:S(2)}) async-start(f32[32,5,128]{2,1,0:T(8,128)} %broadcast_in_dim.23), calls=%async_computation.5 | async-start | bytes 262144 | tf_op jit(solution)/shard_map/all_to_all | solution.py:63

commit v2 on v1

--- a/solution.py
+++ b/solution.py
@@ -25,28 +25,118 @@
     return lax.broadcasted_iota(jnp.int32, (rows, index.shape[-1]), 0) == index
 
 
-def spread_kernel(place_ref, weight_ref, grid_ref):
-    cells, levels = grid_ref.shape
-    at_cell = one_hot(cells, place_ref[0:1, :]).astype(BF16)
+def adjoint_kernel(
+    ens_weight, cells_y, place_ref, first_ref, second_ref, anomaly_ref, sigma_ref, stack_ref, low_ref, high_ref
+):
+    members, slots, cells, levels = anomaly_ref.shape
+    at_cell = one_hot(slots * cells, place_ref[0:1, :]).astype(BF16)
     at_level = one_hot(levels, place_ref[1:2, :])
-    top, low = halves(jnp.where(at_level, weight_ref[...], 0.0))
+    top, low = halves(jnp.where(at_level, first_ref[...] * second_ref[...], 0.0))
     contract = (((1,), (1,)), ((), ()))
-    grid_ref[...] = lax.dot_general(
-        at_cell, top, contract, preferred_element_type=F32
-    ) + lax.dot_general(at_cell, low, contract, preferred_element_type=F32)
-
-
-def sample_kernel(place_ref, field_ref, value_ref):
-    fields, cells, levels = field_ref.shape
-    at_cell = one_hot(cells, place_ref[0:1, :]).astype(BF16)
+    grid = lax.dot_general(at_cell, top, contract, preferred_element_type=F32) + lax.dot_general(
+        at_cell, low, contract, preferred_element_type=F32
+    )
+    parts = [grid[s * cells : (s + 1) * cells] for s in range(slots)]
+    weighted = [ens_weight * part for part in parts]
+
+    def put(k, field):
+        stack_ref[k] = field
+        for x in range(cells // cells_y):
+            first, rim = x * cells_y, 2 * HW
+            low_ref[k, x * rim : (x + 1) * rim, :] = field[first : first + rim]
+            high_ref[k, x * rim : (x + 1) * rim, :] = field[first + cells_y - rim : first + cells_y]
+
+    for k in range(members):
+        put(k, sum(anomaly_ref[k, s].astype(F32) * weighted[s] for s in range(slots)))
+    put(members, STATIC_WEIGHT * sigma_ref[...] * sum(parts))
+
+
+def forward_kernel(
+    ens_weight,
+    share,
+    x_ref,
+    place_ref,
+    above_ref,
+    stack_ref,
+    below_ref,
+    y_ref,
+    z_ref,
+    anomaly_ref,
+    sigma_ref,
+    field_ref,
+    value_ref,
+    wide_ref,
+    held_ref,
+):
+    members, slots, cells, levels = anomaly_ref.shape
+    cells_x = stack_ref.shape[1]
+    cells_y = cells // cells_x
+    rim = above_ref.shape[1]
+
+    def row(x):
+        if x < rim:
+            return above_ref[:, x]
+        if x < rim + cells_x:
+            return stack_ref[:, x - rim]
+        return below_ref[:, x - rim - cells_x]
+
+    at_cell = one_hot(slots * cells, place_ref[0:1, :]).astype(BF16)
     at_level = one_hot(levels, place_ref[1:2, :])
     contract = (((0,), (0,)), ((), ()))
-    for i in range(fields):
-        top, low = halves(field_ref[i])
+    for which in range(2):
+        for x in range(cells_x):
+            wide_ref[...] = sum(x_ref[which, x, o] * row(x + o) for o in range(2 * HW + 1))
+            held_ref[:, x * cells_y : (x + 1) * cells_y, :] = sum(
+                y_ref[which, o][None] * wide_ref[:, o : o + cells_y, :] for o in range(2 * HW + 1)
+            )
+        top, low = halves(held_ref[...].reshape((members + 1) * cells, levels))
+        z_top, z_low = halves(z_ref[which])
+        smooth = (
+            jnp.dot(top, z_top, preferred_element_type=F32)
+            + jnp.dot(top, z_low, preferred_element_type=F32)
+            + jnp.dot(low, z_top, preferred_element_type=F32)
+        ).reshape(members + 1, cells, levels)
+        static = (share * STATIC_WEIGHT) * sigma_ref[...] * smooth[members]
+        parts = []
+        for s in range(slots):
+            part = sum(anomaly_ref[k, s].astype(F32) * smooth[k] for k in range(members))
+            parts.append(ens_weight * part + static)
+        field = jnp.concatenate(parts, axis=0)
+        if which == 0:
+            field_ref[...] = field
+        top, low = halves(field)
         columns = lax.dot_general(
             top, at_cell, contract, preferred_element_type=F32
         ) + lax.dot_general(low, at_cell, contract, preferred_element_type=F32)
-        value_ref[i : i + 1, :] = jnp.sum(jnp.where(at_level, columns, 0.0), axis=0, keepdims=True)
+        value_ref[which : which + 1, :] = jnp.sum(
+            jnp.where(at_level, columns, 0.0), axis=0, keepdims=True
+        )
+
+
+def mix_kernel(products_ref, first_ref, second_ref, total_ref, control_ref, static_ref, field_ref):
+    sums = jnp.sum(jnp.sum(products_ref[...], axis=0), axis=1, keepdims=True)
+    p00, p01, p11, p02, p12 = (sums[i : i + 1] for i in range(5))
+    step0 = p00 / (p00 + p01)
+    keep = 1.0 - step0
+    next_norm = keep * (keep * p00 - 2.0 * step0 * p01) + step0 * step0 * p11
+    beta = next_norm / p00
+    lead = keep + beta
+    own = lead * (lead * p00 - 2.0 * step0 * p01) + step0 * step0 * p11
+    cross = lead * (lead * p01 - step0 * p02) - step0 * (lead * p11 - step0 * p12)
+    step1 = next_norm / (own + cross)
+    mix0 = step0 + step1 * lead
+    mix1 = -step1 * step0
+    members = control_ref.shape[0]
+    for i in range(members):
+        control_ref[i] = mix0 * first_ref[i] + mix1 * second_ref[i]
+    static_ref[...] = mix0 * first_ref[members] + mix1 * second_ref[members]
+    near = total_ref.shape[0]
+    rows = field_ref.shape[0] // near
+    skip = total_ref.shape[1] - 2 * rows
+    for i in range(near):
+        field_ref[i * rows : (i + 1) * rows, :] = (
+            mix0 * total_ref[i, skip : skip + rows, :] + mix1 * total_ref[i, skip + rows :, :]
+        )
 
 
 def groups(size, width, stride):
@@ -126,54 +216,59 @@
     y_rows = y_rows_wide[HW : HW + cells_y]
     y_flip = window(flipped(taper_y), "sy", cells_y, 0)
     x_pair = jnp.stack([x_rows, x_flip])
-    y_pair = jnp.stack([y_rows, y_flip])
+    y_pair = jnp.broadcast_to(
+        jnp.stack([y_rows.T, y_flip.T])[..., None], (2, 2 * HW + 1, cells_y, levels)
+    )
     z_pair = jnp.stack([taper_z, taper_z.T])
 
-    def spread(weights):
-        return pl.pallas_call(
-            spread_kernel,
-            out_shape=jax.ShapeDtypeStruct((slots * cells, levels), F32),
-            compiler_params=pltpu.CompilerParams(vmem_limit_bytes=32 * 2**20),
-        )(place, weights).reshape(slots, cells_x, cells_y, levels)
-
-    def sample(fields):
-        return pl.pallas_call(
-            sample_kernel,
-            out_shape=jax.ShapeDtypeStruct((fields.shape[0], count), F32),
-            compiler_params=pltpu.CompilerParams(vmem_limit_bytes=32 * 2**20),
-        )(place, fields.reshape(fields.shape[0], slots * cells, levels))
-
-    def apply(weights):
-        grid = spread(weights)
-        ens_side = ens_weight * jnp.sum(anomalies.astype(F32) * grid[None], axis=1)
-        static_side = STATIC_WEIGHT * sigma * jnp.sum(grid, axis=0)
-        stack = jnp.concatenate([ens_side, static_side[None]], axis=0)
-        left, right = neighbours(stack[:, :, : 2 * HW], stack[:, :, cells_y - 2 * HW :], "sy")
-        stack = jnp.concatenate([left, stack, right], axis=2)
-        wide_y = cells_y + 2 * HW
-        stack = taps(stack, y_rows_wide, 2, wide_y)
+    params = pltpu.CompilerParams(vmem_limit_bytes=40 * 2**20)
+    packed = anomalies.reshape(local_members, slots, cells, levels)
+    packed_sigma = sigma.reshape(cells, levels)
+    side = cells_x * 2 * HW
+    wide_y = cells_y + 2 * HW
+
+    def apply(first, second):
+        stack, low, high = pl.pallas_call(
+            functools.partial(adjoint_kernel, ens_weight, cells_y),
+            out_shape=(
+                jax.ShapeDtypeStruct((local_members + 1, cells, levels), F32),
+                jax.ShapeDtypeStruct((local_members + 1, side, levels), F32),
+                jax.ShapeDtypeStruct((local_members + 1, side, levels), F32),
+            ),
+            compiler_params=params,
+        )(place, first, second, packed, packed_sigma)
+        left, right = neighbours(low, high, "sy")
+        pieces = [
+            block.reshape(local_members + 1, cells_x, -1, levels) for block in (left, stack, right)
+        ]
+        stack = taps(jnp.concatenate(pieces, axis=2), y_rows_wide, 2, wide_y)
         above, below = neighbours(stack[:, :HW], stack[:, cells_x - HW :], "sx")
         stack = taps(jnp.concatenate([above, stack, below], axis=1), x_rows, 1, cells_x)
         stack = jnp.einsum("bxyk,kl->bxyl", stack, taper_z, precision=HIGH)
         control = stack[:, :, HW : HW + cells_y]
         above, below = neighbours(stack[:, :HW], stack[:, cells_x - HW :], "sx")
-        stack = jnp.concatenate([above, stack, below], axis=1)
-        fields = []
-        for which in range(2):
-            out = taps(stack, x_pair[which], 1, cells_x)
-            out = taps(out, y_pair[which], 2, cells_y)
-            out = jnp.einsum("bxyk,kl->bxyl", out, z_pair[which], precision=HIGH)
-            ens_part = ens_weight * jnp.sum(anomalies.astype(F32) * out[:-1, None], axis=0)
-            fields.append(ens_part + (share * STATIC_WEIGHT) * (sigma * out[-1])[None])
-        sampled = sample(jnp.stack(fields)).reshape(2, rows, levels)
-        return control, fields[0], sampled
-
-    control0, field0, sampled0 = apply(first_weight)
+        whole = pl.BlockSpec(memory_space=pltpu.VMEM)
+        field, sampled = pl.pallas_call(
+            functools.partial(forward_kernel, ens_weight, share),
+            out_shape=(
+                jax.ShapeDtypeStruct((slots * cells, levels), F32),
+                jax.ShapeDtypeStruct((2, count), F32),
+            ),
+            in_specs=[pl.BlockSpec(memory_space=pltpu.SMEM)] + [whole] * 8,
+            scratch_shapes=[
+                pltpu.VMEM((local_members + 1, wide_y, levels), F32),
+                pltpu.VMEM((local_members + 1, cells, levels), F32),
+            ],
+            compiler_params=params,
+        )(x_pair, place, above, stack, below, y_pair, z_pair, packed, packed_sigma)
+        return control, field, sampled.reshape(2, rows, levels)
+
+    control0, field0, sampled0 = apply(obs_weight, innovation.reshape(1, -1))
     part = jnp.sum(gathered(sampled0[0], close, "member", close_groups), axis=0)
-    seen0 = jnp.sum(gathered(part, wide, "member", wide_groups), axis=0)
+    seen0 = lax.psum(part, "member", axis_index_groups=wide_groups)
     obs_rows = obs_weight.reshape(rows, levels)
     weight1 = obs_rows * seen0
-    control1, field1, sampled1 = apply(weight1.reshape(1, -1))
+    control1, field1, sampled1 = apply(obs_weight, seen0.reshape(1, -1))
 
     flat = jnp.concatenate(
         [
@@ -188,8 +283,6 @@
     obs_chunk = rows // near
     seen = total[:, : 3 * obs_chunk].reshape(near, 3, obs_chunk, levels)
     flip0, seen1, flip1 = (seen[:, i].reshape(rows, levels) for i in range(3))
-    fields = total[:, 3 * obs_chunk :].reshape(near, 2, -1, levels)
-    total0, total1 = (fields[:, i].reshape(slots, cells_x, cells_y, levels) for i in range(2))
 
     weight0 = first_weight.reshape(rows, levels)
     weight2 = obs_rows * seen1
@@ -206,22 +299,27 @@
         ]
     )
     regions = lax.axis_size("sx") * lax.axis_size("sy")
-    products = jnp.sum(gathered(products, regions, ("sx", "sy")), axis=(0, 2))
-    p00, p01, p11, p02, p12 = (products[i] for i in range(5))
-
-    step0 = p00 / (p00 + p01)
-    keep = 1.0 - step0
-    next_norm = keep * (keep * p00 - 2.0 * step0 * p01) + step0 * step0 * p11
-    beta = next_norm / p00
-    lead = keep + beta
-    own = lead * (lead * p00 - 2.0 * step0 * p01) + step0 * step0 * p11
-    cross = lead * (lead * p01 - step0 * p02) - step0 * (lead * p11 - step0 * p12)
-    step1 = next_norm / (own + cross)
-    mix0 = step0 + step1 * lead
-    mix1 = -step1 * step0
-    control = mix0 * control0 + mix1 * control1
-    increment = mix0 * total0 + mix1 * total1
-    return control[:-1], control[-1], increment
+    products = gathered(products, regions, ("sx", "sy"))
+    control, static, increment = pl.pallas_call(
+        mix_kernel,
+        out_shape=(
+            jax.ShapeDtypeStruct((local_members, cells, levels), F32),
+            jax.ShapeDtypeStruct((cells, levels), F32),
+            jax.ShapeDtypeStruct((slots * cells, levels), F32),
+        ),
+        compiler_params=params,
+    )(
+        products,
+        control0.reshape(-1, cells, levels),
+        control1.reshape(-1, cells, levels),
+        total,
+    )
+    shape = (cells_x, cells_y, levels)
+    return (
+        control.reshape((local_members,) + shape),
+        static.reshape(shape),
+        increment.reshape((slots,) + shape),
+    )
 
 
 def solution(mesh):

time: 239 us -> 223 us (0.933)
  starting transfers between devices: 53.4 us -> 63.2 us
  between operations: 8.83 us -> 1.08 us
  blocking collectives: 116 us -> 109 us
  waiting for transfers between devices: 39.3 us -> 32.7 us
  Pallas kernels: 2.89 us -> 7.92 us
  other arithmetic: 5.67 us -> 1.89 us
  local copies, waits for them, and re-layouts: 8.55 us -> 5.25 us
    all_to_all x5 -> x4, blocking collectives: 116 us -> 76.7 us  [exchange(): lax.all_to_all(blocks, axis, 0, 0, axis_index_groups=index_groups, tiled=...]
    psum x0 -> x1, blocking collectives: none -> 32 us  [body(): seen0 = lax.psum(part, 'member', axis_index_groups=wide_groups)]
    ppermute x6, starting transfers between devices: 22.6 us -> 32.5 us  [neighbours(): lax.ppermute(high_side, axis, up)]
    pallas_call x4 -> x5, Pallas kernels: 2.89 us -> 7.92 us  [the longest x2 5.7 us: apply(): pl.pallas_call(functools.partial(forward_kernel, ens_weight, share), out_...]
    ppermute x6, waiting for transfers between devices: 24.1 us -> 20.1 us  [neighbours(): lax.ppermute(low_side, axis, down)]
    ppermute x6, waiting for transfers between devices: 7.56 us -> 4.91 us  [neighbours(): lax.ppermute(high_side, axis, up)]
    slice x10 -> x3, local copies, waits for them, and re-layouts: 2.46 us -> 0.07 us  [the longest x2 0.06 us: apply(): control = stack[:, :, HW:HW + cells_y]]
where the time goes in v2:
time: 223 us; the launch traced here: 222 us
  blocking collectives  109 us (49%)
  starting transfers between devices  63.2 us (28%)
  waiting for transfers between devices  32.7 us (15%)
  Pallas kernels  7.92 us (4%)
  local copies, waits for them, and re-layouts  5.25 us (2%)
    all_to_all x4, blocking collectives, exchange(): lax.all_to_all(blocks, axis, 0, 0, axis_index_groups=index_groups, tiled=...  76.7 us
    ppermute x6, starting transfers between devices, neighbours(): lax.ppermute(high_side, axis, up)  32.5 us
    psum x1, blocking collectives, body(): seen0 = lax.psum(part, 'member', axis_index_groups=wide_groups)  32 us
    ppermute x6, waiting for transfers between devices, neighbours(): lax.ppermute(low_side, axis, down)  20.1 us
    ppermute x6, starting transfers between devices, neighbours(): lax.ppermute(low_side, axis, down)  19.8 us
    all_to_all x1, starting transfers between devices, exchange(): lax.all_to_all(blocks, axis, 0, 0, axis_index_groups=index_groups, tiled=...  10.9 us
    all_to_all x1, waiting for transfers between devices, exchange(): lax.all_to_all(blocks, axis, 0, 0, axis_index_groups=index_groups, tiled=...  7.67 us
    pallas_call x2, Pallas kernels, apply(): pl.pallas_call(functools.partial(forward_kernel, ens_weight, share), out_...  5.7 us
  transfers between devices with their start and end apart: 13, of which 11 were waited for; matrix products, arithmetic and copies ran while one was open for 0% of the time, Pallas kernels for 0%

profile of v2, /device:TPU:1, one launch (start us, length us, event | category | flops | bytes accessed | tf_op | source)
XLA Modules:
  0.0 221.8 jit_solution(7612752514501382767)
XLA Ops:
  0.6 0.8 bitcast_add_fusion
  1.5 0.6 copy-done.3
  2.1 1.0 copy-done
  3.1 0.6 shard_map.112
  3.8 5.7 %collective-permute-start = (f32[9,24,128]{2,1,0:T(8,128)S(1)}, f32[9,24,128]{2,1,0:T(8,128)S(1)}, u32[]{:S(2)}, u32[]{:S(2)}) collective-permute-start(f32[9,24,128]{2,1,0:T(8,128)S(1)} %get-tuple-element.16), channel_id=1, source_target_pairs={{0,1},{1,2},{2,3},{3,4},{4,5},{5,6},{6,7},{8,9},{9,10},{10,11},{11... | collective-permute-start | bytes 331784 | tf_op jit(solution)/shard_map/ppermute | solution.py:164
  9.4 1.3 collective-permute-start.1
  10.8 0.7 copy-done.6
  11.6 0.7 copy-done.7
  12.5 4.0 %collective-permute-done.1 = f32[9,24,128]{2,1,0:T(8,128)S(1)} collective-permute-done((f32[9,24,128]{2,1,0:T(8,128)S(1)}, f32[9,24,128]{2,1,0:T(8,128)S(1)}, u32[]{:S(2)}, u32[]{:S(2)}) %collective-permute-start.1) | collective-permute-done | bytes 110624 | tf_op jit(solution)/shard_map/ppermute | solution.py:164
  16.6 0.4 fusion.57
  17.0 4.3 %collective-permute-start.2 = (f32[9,3,22,128]{3,2,1,0:T(8,128)S(1)}, f32[9,3,22,128]{3,2,1,0:T(8,128)S(1)}, u32[]{:S(2)}, u32[]{:S(2)}) collective-permute-start(f32[9,3,22,128]{3,2,1,0:T(8,128)S(1)} %get-tuple-element.40), channel_id=1, source_target_pairs={{0,8},{8,16},{16,24},{1,9},{9,17},{17,25},{2,10},{10,18},{18,26},{... | collective-permute-start | bytes 912392 | tf_op jit(solution)/shard_map/ppermute | solution.py:164
  21.3 10.9 %collective-permute-start.3 = (f32[9,3,22,128]{3,2,1,0:T(8,128)S(1)}, f32[9,3,22,128]{3,2,1,0:T(8,128)S(1)}, u32[]{:S(2)}, u32[]{:S(2)}) collective-permute-start(f32[9,3,22,128]{3,2,1,0:T(8,128)S(1)} %get-tuple-element.41), channel_id=1, source_target_pairs={{8,0},{16,8},{24,16},{9,1},{17,9},{25,17},{10,2},{18,10},{26,18},{... | collective-permute-start | bytes 912392 | tf_op jit(solution)/shard_map/ppermute | solution.py:164
  32.3 0.1 copy.36
  32.4 0.1 copy.37
  32.5 0.1 copy.38
  32.7 0.8 collective-permute-done.3
  33.5 0.6 fusion.23.stack_ref
  34.1 2.4 %collective-permute-start.5 = (f32[9,3,22,128]{3,2,1,0:T(8,128)S(1)}, f32[9,3,22,128]{3,2,1,0:T(8,128)S(1)}, u32[]{:S(2)}, u32[]{:S(2)}) collective-permute-start(f32[9,3,22,128]{3,2,1,0:T(8,128)S(1)} %get-tuple-element.38), channel_id=1, source_target_pairs={{8,0},{16,8},{24,16},{9,1},{17,9},{25,17},{10,2},{18,10},{26,18},{... | collective-permute-start | bytes 912392 | tf_op jit(solution)/shard_map/ppermute | solution.py:164
  36.6 3.3 %collective-permute-start.4 = (f32[9,3,22,128]{3,2,1,0:T(8,128)S(1)}, f32[9,3,22,128]{3,2,1,0:T(8,128)S(1)}, u32[]{:S(2)}, u32[]{:S(2)}) collective-permute-start(f32[9,3,22,128]{3,2,1,0:T(8,128)S(1)} %get-tuple-element.39), channel_id=1, source_target_pairs={{0,8},{8,16},{16,24},{1,9},{9,17},{17,25},{2,10},{10,18},{18,26},{... | collective-permute-start | bytes 912392 | tf_op jit(solution)/shard_map/ppermute | solution.py:164
  39.9 2.8 %collective-permute-done.5.below_ref = f32[9,3,22,128]{3,2,1,0:T(8,128)S(1)} collective-permute-done((f32[9,3,22,128]{3,2,1,0:T(8,128)S(1)}, f32[9,3,22,128]{3,2,1,0:T(8,128)S(1)}, u32[]{:S(2)}, u32[]{:S(2)}) %collective-permute-start.5) | collective-permute-done | bytes 304160 | tf_op jit(solution)/shard_map/ppermute | solution.py:164
  42.7 1.2 collective-permute-done.4.above_ref
  44.0 2.8 %shard_map.113 = (f32[192,128]{1,0:T(8,128)S(1)}, f32[2,2048]{1,0:T(2,128)S(1)}) custom-call(f32[2,4,7]{2,1,0:T(4,128)S(1)} %pad_maximum_fusion.8.x_ref, s32[2,2048]{1,0:T(2,128)S(1)} %pad_add_fusion.place_ref, f32[9,3,22,128]{3,2,1,0:T(8,128)S(1)} %collective-permute-done.4.above_ref, f32[9,4,22,128]{3,2,1,0:T(8,128)S(1)} %fusion.23.stack_ref, ...), custom_call_target="tpu_custom_call" | custom-call | tf_op jit(solution)/shard_map/pallas_call | solution.py:251
  46.9 6.9 %all_to_all.25 = f32[4,16,128]{2,1,0:T(8,128)S(1)} all-to-all(f32[4,16,128]{2,1,0:T(8,128)S(1)} %broadcast_in_dim.14), channel_id=1, replica_groups={{0,32,64,96},{128,160,192,224},{256,288,320,352},{384,416,448,480},{512..., dimensions={0} | all-to-all | bytes 65536 | tf_op jit(solution)/shard_map/all_to_all | solution.py:153
  53.7 32.0 %psum.7 = f32[16,128]{1,0:T(8,128)S(1)} all-reduce(f32[16,128]{1,0:T(8,128)S(1)} %reduce_sum.72), channel_id=1, replica_groups={{0,128,256,384,512,640,768,896},{32,160,288,416,544,672,800,928},{64,19..., use_global_device_ids=true, to_apply=%region_1.2 | all-reduce | flops 2048 | bytes 16384 | tf_op jit(solution)/shard_map/psum | solution.py:268
  85.7 0.6 shard_map.114
  86.4 5.3 %collective-permute-start.6 = (f32[9,24,128]{2,1,0:T(8,128)S(1)}, f32[9,24,128]{2,1,0:T(8,128)S(1)}, u32[]{:S(2)}, u32[]{:S(2)}) collective-permute-start(f32[9,24,128]{2,1,0:T(8,128)S(1)} %get-tuple-element.20), channel_id=1, source_target_pairs={{0,1},{1,2},{2,3},{3,4},{4,5},{5,6},{6,7},{8,9},{9,10},{10,11},{11... | collective-permute-start | bytes 331784 | tf_op jit(solution)/shard_map/ppermute | solution.py:164
  91.7 1.3 collective-permute-start.7
  93.0 0.4 collective-permute-done.6
  93.4 5.2 %collective-permute-done.7 = f32[9,24,128]{2,1,0:T(8,128)S(1)} collective-permute-done((f32[9,24,128]{2,1,0:T(8,128)S(1)}, f32[9,24,128]{2,1,0:T(8,128)S(1)}, u32[]{:S(2)}, u32[]{:S(2)}) %collective-permute-start.7) | collective-permute-done | bytes 110624 | tf_op jit(solution)/shard_map/ppermute | solution.py:164
  98.8 0.4 fusion.45
  99.3 10.4 %collective-permute-start.8 = (f32[9,3,22,128]{3,2,1,0:T(8,128)S(1)}, f32[9,3,22,128]{3,2,1,0:T(8,128)S(1)}, u32[]{:S(2)}, u32[]{:S(2)}) collective-permute-start(f32[9,3,22,128]{3,2,1,0:T(8,128)S(1)} %get-tuple-element.36), channel_id=1, source_target_pairs={{0,8},{8,16},{16,24},{1,9},{9,17},{17,25},{2,10},{10,18},{18,26},{... | collective-permute-start | bytes 912392 | tf_op jit(solution)/shard_map/ppermute | solution.py:164
  109.6 1.9 collective-permute-start.9
  111.6 2.1 collective-permute-done.8
  113.7 4.4 %collective-permute-done.9 = f32[9,3,22,128]{3,2,1,0:T(8,128)S(1)} collective-permute-done((f32[9,3,22,128]{3,2,1,0:T(8,128)S(1)}, f32[9,3,22,128]{3,2,1,0:T(8,128)S(1)}, u32[]{:S(2)}, u32[]{:S(2)}) %collective-permute-start.9) | collective-permute-done | bytes 304160 | tf_op jit(solution)/shard_map/ppermute | solution.py:164
  118.1 0.5 fusion.4.stack_ref
  118.7 1.9 collective-permute-start.11
  120.6 3.6 %collective-permute-start.10 = (f32[9,3,22,128]{3,2,1,0:T(8,128)S(1)}, f32[9,3,22,128]{3,2,1,0:T(8,128)S(1)}, u32[]{:S(2)}, u32[]{:S(2)}) collective-permute-start(f32[9,3,22,128]{3,2,1,0:T(8,128)S(1)} %get-tuple-element.35), channel_id=1, source_target_pairs={{0,8},{8,16},{16,24},{1,9},{9,17},{17,25},{2,10},{10,18},{18,26},{... | collective-permute-start | bytes 912392 | tf_op jit(solution)/shard_map/ppermute | solution.py:164
  124.3 2.9 %collective-permute-done.11.below_ref = f32[9,3,22,128]{3,2,1,0:T(8,128)S(1)} collective-permute-done((f32[9,3,22,128]{3,2,1,0:T(8,128)S(1)}, f32[9,3,22,128]{3,2,1,0:T(8,128)S(1)}, u32[]{:S(2)}, u32[]{:S(2)}) %collective-permute-start.11) | collective-permute-done | bytes 304160 | tf_op jit(solution)/shard_map/ppermute | solution.py:164
  127.1 1.2 collective-permute-done.10.above_ref
  128.3 2.9 %shard_map.115 = (f32[192,128]{1,0:T(8,128)S(1)}, f32[2,2048]{1,0:T(2,128)S(1)}) custom-call(f32[2,4,7]{2,1,0:T(4,128)S(1)} %pad_maximum_fusion.8.x_ref, s32[2,2048]{1,0:T(2,128)S(1)} %pad_add_fusion.place_ref, f32[9,3,22,128]{3,2,1,0:T(8,128)S(1)} %collective-permute-done.10.above_ref, f32[9,4,22,128]{3,2,1,0:T(8,128)S(1)} %fusion.4.stack_ref, ...), custom_call_target="tpu_custom_call" | custom-call | tf_op jit(solution)/shard_map/pallas_call | solution.py:251
  131.2 0.3 concatenate.57
  131.5 16.6 %all_to_all.26 = f32[8,54,128]{2,1,0:T(8,128)S(1)} all-to-all(f32[8,54,128]{2,1,0:T(8,128)S(1)} %concatenate.57), channel_id=1, replica_groups={{0,32,64,96,128,160,192,224},{256,288,320,352,384,416,448,480},{512,544..., dimensions={0} | all-to-all | bytes 442368 | tf_op jit(solution)/shard_map/all_to_all | solution.py:153
  148.2 34.6 %all_to_all.27 = f32[4,54,128]{2,1,0:T(8,128)S(1)} all-to-all(f32[4,54,128]{2,1,0:T(8,128)S(1)} %broadcast_in_dim.15), channel_id=1, replica_groups={{0,256,512,768},{32,288,544,800},{64,320,576,832},{96,352,608,864},{128..., dimensions={0} | all-to-all | bytes 221184 | tf_op jit(solution)/shard_map/all_to_all | solution.py:153
  182.8 18.7 %all_to_all.28.total_ref = f32[8,54,128]{2,1,0:T(8,128)S(1)} all-to-all(f32[8,54,128]{2,1,0:T(8,128)S(1)} %broadcast_in_dim.16), channel_id=1, replica_groups={{0,32,64,96,128,160,192,224},{256,288,320,352,384,416,448,480},{512,544..., dimensions={0} | all-to-all | bytes 442368 | tf_op jit(solution)/shard_map/all_to_all | solution.py:153
  201.6 0.7 broadcast_in_dim.17
  202.3 10.9 %all-to-all-start.4 = ((f32[32,5,128]{2,1,0:T(8,128)}), f32[32,5,128]{2,1,0:T(8,128)S(1)}, u32[]{:S(2)}, u32[]{:S(2)}) async-start(f32[32,5,128]{2,1,0:T(8,128)} %broadcast_in_dim.17), calls=%async_computation.4 | async-start | bytes 262144 | tf_op jit(solution)/shard_map/all_to_all | solution.py:153
  213.2 7.7 %all-to-all-done.4.products_ref = f32[32,5,128]{2,1,0:T(8,128)S(1)} async-done(((f32[32,5,128]{2,1,0:T(8,128)}), f32[32,5,128]{2,1,0:T(8,128)S(1)}, u32[]{:S(2)}, u32[]{:S(2)}) %all-to-all-start.4) | async-done | bytes 81952 | tf_op jit(solution)/shard_map/all_to_all | solution.py:153
  220.9 0.9 shard_map.116
  (54 shorter events, 1.3 us)
Async XLA Ops:
  0.6 0.8 copy-start.2
  1.4 0.7 copy-start.3
  1.4 0.7 copy-start.4
  2.1 1.0 copy-start
  3.8 8.7 %collective-permute-start = (f32[9,24,128]{2,1,0:T(8,128)S(1)}, f32[9,24,128]{2,1,0:T(8,128)S(1)}, u32[]{:S(2)}, u32[]{:S(2)}) collective-permute-start(f32[9,24,128]{2,1,0:T(8,128)S(1)} %get-tuple-element.16), channel_id=1, source_target_pairs={{0,1},{1,2},{2,3},{3,4},{4,5},{5,6},{6,7},{8,9},{9,10},{10,11},{11... | collective-permute-start | bytes 331784 | tf_op jit(solution)/shard_map/ppermute | solution.py:164
  9.4 7.0 %collective-permute-start.1 = (f32[9,24,128]{2,1,0:T(8,128)S(1)}, f32[9,24,128]{2,1,0:T(8,128)S(1)}, u32[]{:S(2)}, u32[]{:S(2)}) collective-permute-start(f32[9,24,128]{2,1,0:T(8,128)S(1)} %get-tuple-element.18), channel_id=1, source_target_pairs={{1,0},{2,1},{3,2},{4,3},{5,4},{6,5},{7,6},{9,8},{10,9},{11,10},{12... | collective-permute-start | bytes 331784 | tf_op jit(solution)/shard_map/ppermute | solution.py:164
  10.8 0.7 copy-start.6
  11.6 0.7 copy-start.7
  17.0 15.5 %copy-start.5 = (f32[128,128]{1,0:T(8,128)S(1)}, f32[128,128]{1,0:T(8,128)}, u32[]{:S(2)}) copy-start(f32[128,128]{1,0:T(8,128)} %param.13) | copy-start | bytes 196612
  17.0 15.7 %collective-permute-start.2 = (f32[9,3,22,128]{3,2,1,0:T(8,128)S(1)}, f32[9,3,22,128]{3,2,1,0:T(8,128)S(1)}, u32[]{:S(2)}, u32[]{:S(2)}) collective-permute-start(f32[9,3,22,128]{3,2,1,0:T(8,128)S(1)} %get-tuple-element.40), channel_id=1, source_target_pairs={{0,8},{8,16},{16,24},{1,9},{9,17},{17,25},{2,10},{10,18},{18,26},{... | collective-permute-start | bytes 912392 | tf_op jit(solution)/shard_map/ppermute | solution.py:164
  21.3 12.2 %collective-permute-start.3 = (f32[9,3,22,128]{3,2,1,0:T(8,128)S(1)}, f32[9,3,22,128]{3,2,1,0:T(8,128)S(1)}, u32[]{:S(2)}, u32[]{:S(2)}) collective-permute-start(f32[9,3,22,128]{3,2,1,0:T(8,128)S(1)} %get-tuple-element.41), channel_id=1, source_target_pairs={{8,0},{16,8},{24,16},{9,1},{17,9},{25,17},{10,2},{18,10},{26,18},{... | collective-permute-start | bytes 912392 | tf_op jit(solution)/shard_map/ppermute | solution.py:164
  34.1 9.9 %copy-start.1 = (bf16[8,3,4,16,128]{4,3,2,1,0:T(8,128)(2,1)S(1)}, bf16[8,3,4,16,128]{4,3,2,1,0:T(8,128)(2,1)}, u32[]{:S(2)}) copy-start(bf16[8,3,4,16,128]{4,3,2,1,0:T(8,128)(2,1)} %param.9) | copy-start | bytes 1179652
  34.1 8.6 %collective-permute-start.5 = (f32[9,3,22,128]{3,2,1,0:T(8,128)S(1)}, f32[9,3,22,128]{3,2,1,0:T(8,128)S(1)}, u32[]{:S(2)}, u32[]{:S(2)}) collective-permute-start(f32[9,3,22,128]{3,2,1,0:T(8,128)S(1)} %get-tuple-element.38), channel_id=1, source_target_pairs={{8,0},{16,8},{24,16},{9,1},{17,9},{25,17},{10,2},{18,10},{26,18},{... | collective-permute-start | bytes 912392 | tf_op jit(solution)/shard_map/ppermute | solution.py:164
  36.6 7.3 %collective-permute-start.4 = (f32[9,3,22,128]{3,2,1,0:T(8,128)S(1)}, f32[9,3,22,128]{3,2,1,0:T(8,128)S(1)}, u32[]{:S(2)}, u32[]{:S(2)}) collective-permute-start(f32[9,3,22,128]{3,2,1,0:T(8,128)S(1)} %get-tuple-element.39), channel_id=1, source_target_pairs={{0,8},{8,16},{16,24},{1,9},{9,17},{17,25},{2,10},{10,18},{18,26},{... | collective-permute-start | bytes 912392 | tf_op jit(solution)/shard_map/ppermute | solution.py:164
  86.4 7.0 %collective-permute-start.6 = (f32[9,24,128]{2,1,0:T(8,128)S(1)}, f32[9,24,128]{2,1,0:T(8,128)S(1)}, u32[]{:S(2)}, u32[]{:S(2)}) collective-permute-start(f32[9,24,128]{2,1,0:T(8,128)S(1)} %get-tuple-element.20), channel_id=1, source_target_pairs={{0,1},{1,2},{2,3},{3,4},{4,5},{5,6},{6,7},{8,9},{9,10},{10,11},{11... | collective-permute-start | bytes 331784 | tf_op jit(solution)/shard_map/ppermute | solution.py:164
  91.7 7.0 %collective-permute-start.7 = (f32[9,24,128]{2,1,0:T(8,128)S(1)}, f32[9,24,128]{2,1,0:T(8,128)S(1)}, u32[]{:S(2)}, u32[]{:S(2)}) collective-permute-start(f32[9,24,128]{2,1,0:T(8,128)S(1)} %get-tuple-element.22), channel_id=1, source_target_pairs={{1,0},{2,1},{3,2},{4,3},{5,4},{6,5},{7,6},{9,8},{10,9},{11,10},{12... | collective-permute-start | bytes 331784 | tf_op jit(solution)/shard_map/ppermute | solution.py:164
  99.3 14.4 %collective-permute-start.8 = (f32[9,3,22,128]{3,2,1,0:T(8,128)S(1)}, f32[9,3,22,128]{3,2,1,0:T(8,128)S(1)}, u32[]{:S(2)}, u32[]{:S(2)}) collective-permute-start(f32[9,3,22,128]{3,2,1,0:T(8,128)S(1)} %get-tuple-element.36), channel_id=1, source_target_pairs={{0,8},{8,16},{16,24},{1,9},{9,17},{17,25},{2,10},{10,18},{18,26},{... | collective-permute-start | bytes 912392 | tf_op jit(solution)/shard_map/ppermute | solution.py:164
  109.6 8.4 %collective-permute-start.9 = (f32[9,3,22,128]{3,2,1,0:T(8,128)S(1)}, f32[9,3,22,128]{3,2,1,0:T(8,128)S(1)}, u32[]{:S(2)}, u32[]{:S(2)}) collective-permute-start(f32[9,3,22,128]{3,2,1,0:T(8,128)S(1)} %get-tuple-element.37), channel_id=1, source_target_pairs={{8,0},{16,8},{24,16},{9,1},{17,9},{25,17},{10,2},{18,10},{26,18},{... | collective-permute-start | bytes 912392 | tf_op jit(solution)/shard_map/ppermute | solution.py:164
  118.7 8.4 %collective-permute-start.11 = (f32[9,3,22,128]{3,2,1,0:T(8,128)S(1)}, f32[9,3,22,128]{3,2,1,0:T(8,128)S(1)}, u32[]{:S(2)}, u32[]{:S(2)}) collective-permute-start(f32[9,3,22,128]{3,2,1,0:T(8,128)S(1)} %get-tuple-element.34), channel_id=1, source_target_pairs={{8,0},{16,8},{24,16},{9,1},{17,9},{25,17},{10,2},{18,10},{26,18},{... | collective-permute-start | bytes 912392 | tf_op jit(solution)/shard_map/ppermute | solution.py:164
  120.6 7.7 %collective-permute-start.10 = (f32[9,3,22,128]{3,2,1,0:T(8,128)S(1)}, f32[9,3,22,128]{3,2,1,0:T(8,128)S(1)}, u32[]{:S(2)}, u32[]{:S(2)}) collective-permute-start(f32[9,3,22,128]{3,2,1,0:T(8,128)S(1)} %get-tuple-element.35), channel_id=1, source_target_pairs={{0,8},{8,16},{16,24},{1,9},{9,17},{17,25},{2,10},{10,18},{18,26},{... | collective-permute-start | bytes 912392 | tf_op jit(solution)/shard_map/ppermute | solution.py:164
  202.3 18.6 %all-to-all-start.4 = ((f32[32,5,128]{2,1,0:T(8,128)}), f32[32,5,128]{2,1,0:T(8,128)S(1)}, u32[]{:S(2)}, u32[]{:S(2)}) async-start(f32[32,5,128]{2,1,0:T(8,128)} %broadcast_in_dim.17), calls=%async_computation.4 | async-start | bytes 262144 | tf_op jit(solution)/shard_map/all_to_all | solution.py:153

commit v3 on v2

--- a/solution.py
+++ b/solution.py
@@ -25,12 +25,28 @@
     return lax.broadcasted_iota(jnp.int32, (rows, index.shape[-1]), 0) == index
 
 
+def observed(slot_ref, index_ref, slots, cells, levels):
+    index = index_ref[...]
+    column = lax.shift_right_logical(index, levels.bit_length() - 1)
+    at_cell = one_hot(slots * cells, slot_ref[...] * cells + column).astype(BF16)
+    return at_cell, one_hot(levels, index - column * levels)
+
+
 def adjoint_kernel(
-    ens_weight, cells_y, place_ref, first_ref, second_ref, anomaly_ref, sigma_ref, stack_ref, low_ref, high_ref
+    ens_weight,
+    cells_y,
+    slot_ref,
+    index_ref,
+    first_ref,
+    second_ref,
+    anomaly_ref,
+    sigma_ref,
+    stack_ref,
+    low_ref,
+    high_ref,
 ):
     members, slots, cells, levels = anomaly_ref.shape
-    at_cell = one_hot(slots * cells, place_ref[0:1, :]).astype(BF16)
-    at_level = one_hot(levels, place_ref[1:2, :])
+    at_cell, at_level = observed(slot_ref, index_ref, slots, cells, levels)
     top, low = halves(jnp.where(at_level, first_ref[...] * second_ref[...], 0.0))
     contract = (((1,), (1,)), ((), ()))
     grid = lax.dot_general(at_cell, top, contract, preferred_element_type=F32) + lax.dot_general(
@@ -55,10 +71,9 @@
     ens_weight,
     share,
     x_ref,
-    place_ref,
-    above_ref,
+    slot_ref,
+    index_ref,
     stack_ref,
-    below_ref,
     y_ref,
     z_ref,
     anomaly_ref,
@@ -69,23 +84,13 @@
     held_ref,
 ):
     members, slots, cells, levels = anomaly_ref.shape
-    cells_x = stack_ref.shape[1]
+    cells_x = x_ref.shape[1]
     cells_y = cells // cells_x
-    rim = above_ref.shape[1]
-
-    def row(x):
-        if x < rim:
-            return above_ref[:, x]
-        if x < rim + cells_x:
-            return stack_ref[:, x - rim]
-        return below_ref[:, x - rim - cells_x]
-
-    at_cell = one_hot(slots * cells, place_ref[0:1, :]).astype(BF16)
-    at_level = one_hot(levels, place_ref[1:2, :])
+    at_cell, at_level = observed(slot_ref, index_ref, slots, cells, levels)
     contract = (((0,), (0,)), ((), ()))
     for which in range(2):
         for x in range(cells_x):
-            wide_ref[...] = sum(x_ref[which, x, o] * row(x + o) for o in range(2 * HW + 1))
+            wide_ref[...] = sum(x_ref[which, x, o] * stack_ref[:, x + o] for o in range(2 * HW + 1))
             held_ref[:, x * cells_y : (x + 1) * cells_y, :] = sum(
                 y_ref[which, o][None] * wide_ref[:, o : o + cells_y, :] for o in range(2 * HW + 1)
             )
@@ -113,6 +118,31 @@
         )
 
 
+def product_kernel(total_ref, weight_ref, first_ref, seen_ref, products_ref):
+    near = total_ref.shape[0]
+    rows, levels = weight_ref.shape
+    part = rows // near
+
+    def sampled(which):
+        pieces = [total_ref[i, which * part : (which + 1) * part, :] for i in range(near)]
+        return jnp.concatenate(pieces, axis=0)
+
+    flip0, seen1, flip1 = (sampled(which) for which in range(3))
+    weight0 = weight_ref[...] * first_ref[...]
+    weight1 = weight_ref[...] * seen_ref[...]
+    weight2 = weight_ref[...] * seen1
+    pairs = (
+        (weight0, flip0),
+        (weight1, flip0),
+        (weight1, flip1),
+        (weight2, flip0),
+        (weight2, flip1),
+    )
+    sums = [jnp.sum(a * b, axis=0, keepdims=True) for a, b in pairs]
+    sums.append(jnp.zeros((products_ref.shape[1] - len(pairs), levels), F32))
+    products_ref[...] = jnp.broadcast_to(jnp.concatenate(sums, axis=0)[None], products_ref.shape)
+
+
 def mix_kernel(products_ref, first_ref, second_ref, total_ref, control_ref, static_ref, field_ref):
     sums = jnp.sum(jnp.sum(products_ref[...], axis=0), axis=1, keepdims=True)
     p00, p01, p11, p02, p12 = (sums[i : i + 1] for i in range(5))
@@ -164,6 +194,30 @@
     return lax.ppermute(high_side, axis, up), lax.ppermute(low_side, axis, down)
 
 
+def paired(low_side, high_side, axis):
+    count = lax.axis_size(axis)
+    place = lax.axis_index(axis)
+    even = [(i, i + 1) for i in range(0, count - 1, 2)]
+    odd = [(i, i + 1) for i in range(1, count - 1, 2)]
+    upper = lax.rem(place, 2) == 1
+    far = lax.ppermute(jnp.where(upper, high_side, low_side), axis, odd + [(j, i) for i, j in odd])
+    close = lax.ppermute(jnp.where(upper, low_side, high_side), axis, even + [(j, i) for i, j in even])
+    return jnp.where(upper, close, far), jnp.where(upper, far, close)
+
+
+def widened(block, extra, axis):
+    size = block.shape[1]
+    place = lax.axis_index(axis)
+    upper = place >= 2
+    edge = jnp.where(upper, block[:, :extra], block[:, size - extra :])
+    beyond = lax.ppermute(edge, axis, [(0, 2), (2, 0), (1, 3), (3, 1)])
+    above, below = paired(block, block, axis)
+    none = jnp.zeros_like(beyond)
+    return jnp.concatenate(
+        [jnp.where(upper, beyond, none), above, block, below, jnp.where(upper, none, beyond)], axis=1
+    )
+
+
 def taps(field, table, dim, count):
     total = None
     for offset in range(2 * HW + 1):
@@ -203,14 +257,13 @@
     close_groups = groups(member_devices, close, 1)
     wide_groups = groups(member_devices, wide, close)
 
-    index_flat = obs_index.reshape(1, -1)
-    place = jnp.concatenate(
-        [obs_slot.reshape(1, -1) * cells + index_flat // levels, index_flat % levels], axis=0
-    )
+    index = obs_index.reshape(1, -1)
+    slot = obs_slot.reshape(1, -1)
     obs_weight = obs_inverse.reshape(1, -1)
-    first_weight = obs_weight * innovation.reshape(1, -1)
-
-    x_rows = window(taper_x, "sx", cells_x, 0)
+    first = innovation.reshape(1, -1)
+
+    x_rows_wide = window(taper_x, "sx", cells_x, HW)
+    x_rows = x_rows_wide[HW : HW + cells_x]
     x_flip = window(flipped(taper_x), "sx", cells_x, 0)
     y_rows_wide = window(taper_y, "sy", cells_y, HW)
     y_rows = y_rows_wide[HW : HW + cells_y]
@@ -227,7 +280,7 @@
     side = cells_x * 2 * HW
     wide_y = cells_y + 2 * HW
 
-    def apply(first, second):
+    def apply(first, second, room):
         stack, low, high = pl.pallas_call(
             functools.partial(adjoint_kernel, ens_weight, cells_y),
             out_shape=(
@@ -235,18 +288,16 @@
                 jax.ShapeDtypeStruct((local_members + 1, side, levels), F32),
                 jax.ShapeDtypeStruct((local_members + 1, side, levels), F32),
             ),
-            compiler_params=params,
-        )(place, first, second, packed, packed_sigma)
+            compiler_params=pltpu.CompilerParams(vmem_limit_bytes=room * 2**20),
+        )(slot, index, first, second, packed, packed_sigma)
         left, right = neighbours(low, high, "sy")
         pieces = [
             block.reshape(local_members + 1, cells_x, -1, levels) for block in (left, stack, right)
         ]
         stack = taps(jnp.concatenate(pieces, axis=2), y_rows_wide, 2, wide_y)
-        above, below = neighbours(stack[:, :HW], stack[:, cells_x - HW :], "sx")
-        stack = taps(jnp.concatenate([above, stack, below], axis=1), x_rows, 1, cells_x)
+        stack = taps(widened(stack, 2 * HW - cells_x, "sx"), x_rows_wide, 1, cells_x + 2 * HW)
         stack = jnp.einsum("bxyk,kl->bxyl", stack, taper_z, precision=HIGH)
-        control = stack[:, :, HW : HW + cells_y]
-        above, below = neighbours(stack[:, :HW], stack[:, cells_x - HW :], "sx")
+        control = stack[:, HW : HW + cells_x, HW : HW + cells_y]
         whole = pl.BlockSpec(memory_space=pltpu.VMEM)
         field, sampled = pl.pallas_call(
             functools.partial(forward_kernel, ens_weight, share),
@@ -254,52 +305,32 @@
                 jax.ShapeDtypeStruct((slots * cells, levels), F32),
                 jax.ShapeDtypeStruct((2, count), F32),
             ),
-            in_specs=[pl.BlockSpec(memory_space=pltpu.SMEM)] + [whole] * 8,
+            in_specs=[pl.BlockSpec(memory_space=pltpu.SMEM)] + [whole] * 7,
             scratch_shapes=[
                 pltpu.VMEM((local_members + 1, wide_y, levels), F32),
                 pltpu.VMEM((local_members + 1, cells, levels), F32),
             ],
             compiler_params=params,
-        )(x_pair, place, above, stack, below, y_pair, z_pair, packed, packed_sigma)
+        )(x_pair, slot, index, stack, y_pair, z_pair, packed, packed_sigma)
         return control, field, sampled.reshape(2, rows, levels)
 
-    control0, field0, sampled0 = apply(obs_weight, innovation.reshape(1, -1))
+    control0, field0, sampled0 = apply(obs_weight, first, 60)
     part = jnp.sum(gathered(sampled0[0], close, "member", close_groups), axis=0)
     seen0 = lax.psum(part, "member", axis_index_groups=wide_groups)
-    obs_rows = obs_weight.reshape(rows, levels)
-    weight1 = obs_rows * seen0
-    control1, field1, sampled1 = apply(obs_weight, seen0.reshape(1, -1))
-
-    flat = jnp.concatenate(
-        [
-            block.reshape(near, -1, levels)
-            for block in (sampled0[1], sampled1[0], sampled1[1], field0, field1)
-        ],
-        axis=1,
-    )
+    control1, field1, sampled1 = apply(obs_weight, seen0.reshape(1, -1), 40)
+
+    blocks = (sampled0[1], sampled1[0], sampled1[1], field0, field1)
+    flat = jnp.concatenate([block.reshape(near, -1, levels) for block in blocks], axis=1)
     chunk = jnp.sum(exchange(flat, "member", near_groups), axis=0)
     chunk = jnp.sum(gathered(chunk, far, "member", far_groups), axis=0)
     total = gathered(chunk, near, "member", near_groups)
-    obs_chunk = rows // near
-    seen = total[:, : 3 * obs_chunk].reshape(near, 3, obs_chunk, levels)
-    flip0, seen1, flip1 = (seen[:, i].reshape(rows, levels) for i in range(3))
-
-    weight0 = first_weight.reshape(rows, levels)
-    weight2 = obs_rows * seen1
-    products = jnp.stack(
-        [
-            jnp.sum(a * b, axis=0)
-            for a, b in (
-                (weight0, flip0),
-                (weight1, flip0),
-                (weight1, flip1),
-                (weight2, flip0),
-                (weight2, flip1),
-            )
-        ]
-    )
     regions = lax.axis_size("sx") * lax.axis_size("sy")
-    products = gathered(products, regions, ("sx", "sy"))
+    products = pl.pallas_call(
+        product_kernel,
+        out_shape=jax.ShapeDtypeStruct((regions, 8, levels), F32),
+        compiler_params=params,
+    )(total, obs_inverse.reshape(rows, levels), innovation.reshape(rows, levels), seen0)
+    products = exchange(products, ("sx", "sy"))
     control, static, increment = pl.pallas_call(
         mix_kernel,
         out_shape=(

time: 223 us -> 209 us (0.937)
  starting transfers between devices: 63.2 us -> 53.5 us
  waiting for transfers between devices: 32.7 us -> 26.5 us
  Pallas kernels: 7.92 us -> 10.5 us
    ppermute x0 -> x6, starting transfers between devices: none -> 30.6 us  [the longest x2 14.4 us: paired(): lax.ppermute(jnp.where(upper, high_side, low_side), axis, odd + [(j, i) f...]
    ppermute x6 -> x2, starting transfers between devices: 32.5 us -> 11.1 us  [neighbours(): lax.ppermute(high_side, axis, up)]
    ppermute x6 -> x2, starting transfers between devices: 19.8 us -> 2.58 us  [neighbours(): lax.ppermute(low_side, axis, down)]
    ppermute x6 -> x2, waiting for transfers between devices: 20.1 us -> 7.07 us  [neighbours(): lax.ppermute(low_side, axis, down)]
    ppermute x0 -> x6, waiting for transfers between devices: none -> 11.3 us  [the longest x2 6.88 us: widened(): beyond = lax.ppermute(edge, axis, [(0, 2), (2, 0), (1, 3), (3, 1)])]
    ppermute x6 -> x2, waiting for transfers between devices: 4.91 us -> 0.43 us  [neighbours(): lax.ppermute(high_side, axis, up)]
    psum x1, blocking collectives: 32 us -> 28.1 us  [body(): seen0 = lax.psum(part, 'member', axis_index_groups=wide_groups)]
    unnamed x17, local copies, waits for them, and re-layouts: 3.13 us -> 0.14 us
  transfers between devices with their start and end apart: 13 -> 11, of which waited for: 11 -> 6; matrix products, arithmetic and copies ran while one was open for 0% -> 2% of each run, Pallas kernels for 0% -> 0%
where the time goes in v3:
time: 209 us; the launch traced here: 208 us
  blocking collectives  107 us (51%)
  starting transfers between devices  53.5 us (26%)
  waiting for transfers between devices  26.5 us (13%)
  Pallas kernels  10.5 us (5%)
  local copies, waits for them, and re-layouts  4.77 us (2%)
  other arithmetic  2.43 us (1%)
  matrix products  2.12 us (1%)
    all_to_all x4, blocking collectives, exchange(): lax.all_to_all(blocks, axis, 0, 0, axis_index_groups=index_groups, tiled=...  78.8 us
    psum x1, blocking collectives, body(): seen0 = lax.psum(part, 'member', axis_index_groups=wide_groups)  28.1 us
    ppermute x2, starting transfers between devices, paired(): lax.ppermute(jnp.where(upper, high_side, low_side), axis, odd + [(j, i) f...  14.4 us
    ppermute x2, starting transfers between devices, paired(): lax.ppermute(jnp.where(upper, low_side, high_side), axis, even + [(j, i)...  11.3 us
    ppermute x2, starting transfers between devices, neighbours(): lax.ppermute(high_side, axis, up)  11.1 us
    all_to_all x1, starting transfers between devices, exchange(): lax.all_to_all(blocks, axis, 0, 0, axis_index_groups=index_groups, tiled=...  9.28 us
    all_to_all x1, waiting for transfers between devices, exchange(): lax.all_to_all(blocks, axis, 0, 0, axis_index_groups=index_groups, tiled=...  7.67 us
    ppermute x2, waiting for transfers between devices, neighbours(): lax.ppermute(low_side, axis, down)  7.07 us
  transfers between devices with their start and end apart: 11, of which 6 were waited for; matrix products, arithmetic and copies ran while one was open for 2% of the time, Pallas kernels for 0%

profile of v3, /device:TPU:1, one launch (start us, length us, event | category | flops | bytes accessed | tf_op | source)
XLA Modules:
  0.0 207.8 jit_solution(3229208748685438643)
XLA Ops:
  0.6 2.5 %shard_map.112 = (f32[9,64,128]{2,1,0:T(8,128)}, f32[9,24,128]{2,1,0:T(8,128)}, f32[9,24,128]{2,1,0:T(8,128)}) custom-call(s32[1,2048]{1,0:T(1,128)} %bitcast.83, s32[1,2048]{1,0:T(1,128)} %bitcast.87, f32[1,2048]{1,0:T(1,128)} %bitcast.93, f32[1,2048]{1,0:T(1,128)} %bitcast.97, bf16[8,3,64,128]{3,2,1,0:T(8,128)(2,1)} %bitcast.71, f32[64,128]{1,0:T(8,128)} %bitcast.79), custom_call_target="tpu_custom_call" | custom-call | tf_op jit(solution)/shard_map/pallas_call | solution.py:284
  3.1 5.8 %collective-permute-start = (f32[9,24,128]{2,1,0:T(8,128)}, f32[9,24,128]{2,1,0:T(8,128)S(1)}, u32[]{:S(2)}, u32[]{:S(2)}) collective-permute-start(f32[9,24,128]{2,1,0:T(8,128)} %get-tuple-element.16), channel_id=1, source_target_pairs={{0,1},{1,2},{2,3},{3,4},{4,5},{5,6},{6,7},{8,9},{9,10},{10,11},{11... | collective-permute-start | bytes 331784 | tf_op jit(solution)/shard_map/ppermute | solution.py:194
  8.9 1.3 collective-permute-start.1
  10.2 0.8 pad_dynamic-slice_fusion.1
  11.0 0.1 slice.226
  11.1 1.0 pad_slice_fusion.6
  12.1 1.0 pad_slice_fusion
  13.1 0.8 pad_dynamic-slice_fusion
  13.9 0.1 copy.21
  14.0 0.1 constant_dynamic-slice_fusion
  14.1 0.1 copy.22
  14.2 0.1 dynamic-slice_bitcast_fusion
  14.3 1.8 collective-permute-done.1
  16.1 1.0 pad_maximum_fusion.22
  17.2 0.4 fusion.69
  17.6 4.3 %collective-permute-start.4 = (f32[9,4,22,128]{3,2,1,0:T(8,128)S(1)}, f32[9,4,22,128]{3,2,1,0:T(8,128)S(1)}, u32[]{:S(2)}, u32[]{:S(2)}) collective-permute-start(f32[9,4,22,128]{3,2,1,0:T(8,128)S(1)} %fusion.69), channel_id=1, source_target_pairs={{8,16},{16,8},{9,17},{17,9},{10,18},{18,10},{11,19},{19,11},{12,20... | collective-permute-start | bytes 1216520 | tf_op jit(solution)/shard_map/ppermute | solution.py:203
  21.9 9.4 %collective-permute-start.3 = (f32[9,4,22,128]{3,2,1,0:T(8,128)S(1)}, f32[9,4,22,128]{3,2,1,0:T(8,128)S(1)}, u32[]{:S(2)}, u32[]{:S(2)}) collective-permute-start(f32[9,4,22,128]{3,2,1,0:T(8,128)S(1)} %fusion.69), channel_id=1, source_target_pairs={{0,8},{16,24},{8,0},{24,16},{1,9},{17,25},{9,1},{25,17},{2,10},{18... | collective-permute-start | bytes 1216520 | tf_op jit(solution)/shard_map/ppermute | solution.py:204
  31.3 1.9 collective-permute-start.2
  33.3 0.1 copy.23
  33.4 6.9 %collective-permute-done.2 = f32[9,2,22,128]{3,2,1,0:T(8,128)S(1)} collective-permute-done((f32[9,2,22,128]{3,2,1,0:T(8,128)S(1)}, f32[9,2,22,128]{3,2,1,0:T(8,128)S(1)}, u32[]{:S(2)}, u32[]{:S(2)}) %collective-permute-start.2) | collective-permute-done | bytes 202784 | tf_op jit(solution)/shard_map/ppermute | solution.py:213
  40.4 0.1 pad_maximum_fusion
  40.6 1.1 fusion.19.stack_ref
  41.6 0.1 broadcast_in_dim.10.y_ref
  41.8 2.8 %shard_map.113 = (f32[192,128]{1,0:T(8,128)S(1)}, f32[2,2048]{1,0:T(2,128)S(1)}) custom-call(f32[2,4,7]{2,1,0:T(4,128)S(1)} %pad_maximum_fusion.26.x_ref, s32[1,2048]{1,0:T(1,128)S(1)} %bitcast.84, s32[1,2048]{1,0:T(1,128)S(1)} %bitcast.88, f32[9,10,22,128]{3,2,1,0:T(8,128)S(1)} %fusion.19.stack_ref, f32[2,7,16,128]{3,2,1,0:T(8,128)S(1)} %broadcast_in_dim.10.y_ref, ...), custom_call_target="tpu_custom_call" | custom-call | tf_op jit(solution)/shard_map/pallas_call | solution.py:302
  44.7 6.9 %all_to_all.25 = f32[4,16,128]{2,1,0:T(8,128)S(1)} all-to-all(f32[4,16,128]{2,1,0:T(8,128)S(1)} %broadcast_in_dim.12), channel_id=1, replica_groups={{0,32,64,96},{128,160,192,224},{256,288,320,352},{384,416,448,480},{512..., dimensions={0} | all-to-all | bytes 65536 | tf_op jit(solution)/shard_map/all_to_all | solution.py:183
  51.5 28.1 %psum.7.seen_ref = f32[16,128]{1,0:T(8,128)S(1)} all-reduce(f32[16,128]{1,0:T(8,128)S(1)} %reduce_sum.27), channel_id=1, replica_groups={{0,128,256,384,512,640,768,896},{32,160,288,416,544,672,800,928},{64,19..., use_global_device_ids=true, to_apply=%region_1.2 | all-reduce | flops 2048 | bytes 16384 | tf_op jit(solution)/shard_map/psum | solution.py:319
  79.6 0.6 shard_map.114
  80.3 5.3 %collective-permute-start.5 = (f32[9,24,128]{2,1,0:T(8,128)S(1)}, f32[9,24,128]{2,1,0:T(8,128)S(1)}, u32[]{:S(2)}, u32[]{:S(2)}) collective-permute-start(f32[9,24,128]{2,1,0:T(8,128)S(1)} %get-tuple-element.20), channel_id=1, source_target_pairs={{0,1},{1,2},{2,3},{3,4},{4,5},{5,6},{6,7},{8,9},{9,10},{10,11},{11... | collective-permute-start | bytes 331784 | tf_op jit(solution)/shard_map/ppermute | solution.py:194
  85.6 1.3 collective-permute-start.6
  86.9 0.4 collective-permute-done.5
  87.3 5.2 %collective-permute-done.6 = f32[9,24,128]{2,1,0:T(8,128)S(1)} collective-permute-done((f32[9,24,128]{2,1,0:T(8,128)S(1)}, f32[9,24,128]{2,1,0:T(8,128)S(1)}, u32[]{:S(2)}, u32[]{:S(2)}) %collective-permute-start.6) | collective-permute-done | bytes 110624 | tf_op jit(solution)/shard_map/ppermute | solution.py:194
  92.6 0.1 pad_maximum_fusion.23
  92.7 0.4 fusion.63
  93.1 3.0 %collective-permute-start.7 = (f32[9,2,22,128]{3,2,1,0:T(8,128)S(1)}, f32[9,2,22,128]{3,2,1,0:T(8,128)S(1)}, u32[]{:S(2)}, u32[]{:S(2)}) collective-permute-start(f32[9,2,22,128]{3,2,1,0:T(8,128)S(1)} %slice_select_fusion), channel_id=1, source_target_pairs={{0,16},{16,0},{8,24},{24,8},{1,17},{17,1},{9,25},{25,9},{2,18},{18... | collective-permute-start | bytes 608264 | tf_op jit(solution)/shard_map/ppermute | solution.py:213
  96.1 10.1 %collective-permute-start.9 = (f32[9,4,22,128]{3,2,1,0:T(8,128)S(1)}, f32[9,4,22,128]{3,2,1,0:T(8,128)S(1)}, u32[]{:S(2)}, u32[]{:S(2)}) collective-permute-start(f32[9,4,22,128]{3,2,1,0:T(8,128)S(1)} %fusion.63), channel_id=1, source_target_pairs={{8,16},{16,8},{9,17},{17,9},{10,18},{18,10},{11,19},{19,11},{12,20... | collective-permute-start | bytes 1216520 | tf_op jit(solution)/shard_map/ppermute | solution.py:203
  106.2 1.9 collective-permute-start.8
  108.2 4.4 %collective-permute-done.9 = f32[9,4,22,128]{3,2,1,0:T(8,128)S(1)} collective-permute-done((f32[9,4,22,128]{3,2,1,0:T(8,128)S(1)}, f32[9,4,22,128]{3,2,1,0:T(8,128)S(1)}, u32[]{:S(2)}, u32[]{:S(2)}) %collective-permute-start.9) | collective-permute-done | bytes 405536 | tf_op jit(solution)/shard_map/ppermute | solution.py:203
  112.7 0.1 pad_maximum_fusion.1
  112.8 1.1 fusion.3.stack_ref
  113.9 2.9 %shard_map.115 = (f32[192,128]{1,0:T(8,128)S(1)}, f32[2,2048]{1,0:T(2,128)S(1)}) custom-call(f32[2,4,7]{2,1,0:T(4,128)S(1)} %pad_maximum_fusion.26.x_ref, s32[1,2048]{1,0:T(1,128)S(1)} %bitcast.86, s32[1,2048]{1,0:T(1,128)S(1)} %bitcast.90, f32[9,10,22,128]{3,2,1,0:T(8,128)S(1)} %fusion.3.stack_ref, f32[2,7,16,128]{3,2,1,0:T(8,128)S(1)} %broadcast_in_dim.10.y_ref, ...), custom_call_target="tpu_custom_call" | custom-call | tf_op jit(solution)/shard_map/pallas_call | solution.py:302
  116.8 0.3 concatenate.73
  117.1 18.8 %all_to_all.26 = f32[8,54,128]{2,1,0:T(8,128)S(1)} all-to-all(f32[8,54,128]{2,1,0:T(8,128)S(1)} %concatenate.73), channel_id=1, replica_groups={{0,32,64,96,128,160,192,224},{256,288,320,352,384,416,448,480},{512,544..., dimensions={0} | all-to-all | bytes 442368 | tf_op jit(solution)/shard_map/all_to_all | solution.py:183
  136.0 34.6 %all_to_all.27 = f32[4,54,128]{2,1,0:T(8,128)S(1)} all-to-all(f32[4,54,128]{2,1,0:T(8,128)S(1)} %broadcast_in_dim.13), channel_id=1, replica_groups={{0,256,512,768},{32,288,544,800},{64,320,576,832},{96,352,608,864},{128..., dimensions={0} | all-to-all | bytes 221184 | tf_op jit(solution)/shard_map/all_to_all | solution.py:183
  170.7 18.5 %all_to_all.28.total_ref = f32[8,54,128]{2,1,0:T(8,128)S(1)} all-to-all(f32[8,54,128]{2,1,0:T(8,128)S(1)} %broadcast_in_dim.14), channel_id=1, replica_groups={{0,32,64,96,128,160,192,224},{256,288,320,352,384,416,448,480},{512,544..., dimensions={0} | all-to-all | bytes 442368 | tf_op jit(solution)/shard_map/all_to_all | solution.py:183
  189.2 0.7 shard_map.116
  189.8 9.3 %all-to-all-start.4 = ((f32[32,8,128]{2,1,0:T(8,128)}), f32[32,8,128]{2,1,0:T(8,128)S(1)}, u32[]{:S(2)}, u32[]{:S(2)}) async-start(f32[32,8,128]{2,1,0:T(8,128)} %shard_map.116), calls=%async_computation.4 | async-start | bytes 262144 | tf_op jit(solution)/shard_map/all_to_all | solution.py:183
  199.2 7.7 %all-to-all-done.4.products_ref = f32[32,8,128]{2,1,0:T(8,128)S(1)} async-done(((f32[32,8,128]{2,1,0:T(8,128)}), f32[32,8,128]{2,1,0:T(8,128)S(1)}, u32[]{:S(2)}, u32[]{:S(2)}) %all-to-all-start.4) | async-done | bytes 131104 | tf_op jit(solution)/shard_map/all_to_all | solution.py:183
  206.9 0.9 shard_map.117
  (48 shorter events, 0.6 us)
Async XLA Ops:
  3.1 14.1 %copy-start.6 = (f32[9,64,128]{2,1,0:T(8,128)S(1)}, f32[9,64,128]{2,1,0:T(8,128)}, u32[]{:S(2)}) copy-start(f32[9,64,128]{2,1,0:T(8,128)} %get-tuple-element.17) | copy-start | bytes 884740
  3.1 11.1 %collective-permute-start = (f32[9,24,128]{2,1,0:T(8,128)}, f32[9,24,128]{2,1,0:T(8,128)S(1)}, u32[]{:S(2)}, u32[]{:S(2)}) collective-permute-start(f32[9,24,128]{2,1,0:T(8,128)} %get-tuple-element.16), channel_id=1, source_target_pairs={{0,1},{1,2},{2,3},{3,4},{4,5},{5,6},{6,7},{8,9},{9,10},{10,11},{11... | collective-permute-start | bytes 331784 | tf_op jit(solution)/shard_map/ppermute | solution.py:194
  8.9 7.2 %collective-permute-start.1 = (f32[9,24,128]{2,1,0:T(8,128)}, f32[9,24,128]{2,1,0:T(8,128)S(1)}, u32[]{:S(2)}, u32[]{:S(2)}) collective-permute-start(f32[9,24,128]{2,1,0:T(8,128)} %get-tuple-element.18), channel_id=1, source_target_pairs={{1,0},{2,1},{3,2},{4,3},{5,4},{6,5},{7,6},{9,8},{10,9},{11,10},{12... | collective-permute-start | bytes 331784 | tf_op jit(solution)/shard_map/ppermute | solution.py:194
  17.2 16.1 %copy-start.7 = (f32[128,128]{1,0:T(8,128)S(1)}, f32[128,128]{1,0:T(8,128)}, u32[]{:S(2)}) copy-start(f32[128,128]{1,0:T(8,128)} %param.13) | copy-start | bytes 196612
  17.6 22.7 %collective-permute-start.4 = (f32[9,4,22,128]{3,2,1,0:T(8,128)S(1)}, f32[9,4,22,128]{3,2,1,0:T(8,128)S(1)}, u32[]{:S(2)}, u32[]{:S(2)}) collective-permute-start(f32[9,4,22,128]{3,2,1,0:T(8,128)S(1)} %fusion.69), channel_id=1, source_target_pairs={{8,16},{16,8},{9,17},{17,9},{10,18},{18,10},{11,19},{19,11},{12,20... | collective-permute-start | bytes 1216520 | tf_op jit(solution)/shard_map/ppermute | solution.py:203
  21.9 18.4 %collective-permute-start.3 = (f32[9,4,22,128]{3,2,1,0:T(8,128)S(1)}, f32[9,4,22,128]{3,2,1,0:T(8,128)S(1)}, u32[]{:S(2)}, u32[]{:S(2)}) collective-permute-start(f32[9,4,22,128]{3,2,1,0:T(8,128)S(1)} %fusion.69), channel_id=1, source_target_pairs={{0,8},{16,24},{8,0},{24,16},{1,9},{17,25},{9,1},{25,17},{2,10},{18... | collective-permute-start | bytes 1216520 | tf_op jit(solution)/shard_map/ppermute | solution.py:204
  31.3 8.9 %collective-permute-start.2 = (f32[9,2,22,128]{3,2,1,0:T(8,128)S(1)}, f32[9,2,22,128]{3,2,1,0:T(8,128)S(1)}, u32[]{:S(2)}, u32[]{:S(2)}) collective-permute-start(f32[9,2,22,128]{3,2,1,0:T(8,128)S(1)} %slice_select_fusion.1), channel_id=1, source_target_pairs={{0,16},{16,0},{8,24},{24,8},{1,17},{17,1},{9,25},{25,9},{2,18},{18... | collective-permute-start | bytes 608264 | tf_op jit(solution)/shard_map/ppermute | solution.py:213
  40.5 1.2 copy-start
  40.5 1.2 copy-start.1
  40.5 1.2 copy-start.2
  40.5 1.2 copy-start.3
  41.6 38.0 %copy-start.4 = (f32[1,1,2048]{2,1,0:T(1,128)S(1)}, f32[1,1,2048]{2,1,0:T(1,128)}, u32[]{:S(2)}) copy-start(f32[1,1,2048]{2,1,0:T(1,128)} %param.15) | copy-start | bytes 24580
  80.3 7.0 %collective-permute-start.5 = (f32[9,24,128]{2,1,0:T(8,128)S(1)}, f32[9,24,128]{2,1,0:T(8,128)S(1)}, u32[]{:S(2)}, u32[]{:S(2)}) collective-permute-start(f32[9,24,128]{2,1,0:T(8,128)S(1)} %get-tuple-element.20), channel_id=1, source_target_pairs={{0,1},{1,2},{2,3},{3,4},{4,5},{5,6},{6,7},{8,9},{9,10},{10,11},{11... | collective-permute-start | bytes 331784 | tf_op jit(solution)/shard_map/ppermute | solution.py:194
  85.6 7.0 %collective-permute-start.6 = (f32[9,24,128]{2,1,0:T(8,128)S(1)}, f32[9,24,128]{2,1,0:T(8,128)S(1)}, u32[]{:S(2)}, u32[]{:S(2)}) collective-permute-start(f32[9,24,128]{2,1,0:T(8,128)S(1)} %get-tuple-element.22), channel_id=1, source_target_pairs={{1,0},{2,1},{3,2},{4,3},{5,4},{6,5},{7,6},{9,8},{10,9},{11,10},{12... | collective-permute-start | bytes 331784 | tf_op jit(solution)/shard_map/ppermute | solution.py:194
  93.1 15.0 %collective-permute-start.7 = (f32[9,2,22,128]{3,2,1,0:T(8,128)S(1)}, f32[9,2,22,128]{3,2,1,0:T(8,128)S(1)}, u32[]{:S(2)}, u32[]{:S(2)}) collective-permute-start(f32[9,2,22,128]{3,2,1,0:T(8,128)S(1)} %slice_select_fusion), channel_id=1, source_target_pairs={{0,16},{16,0},{8,24},{24,8},{1,17},{17,1},{9,25},{25,9},{2,18},{18... | collective-permute-start | bytes 608264 | tf_op jit(solution)/shard_map/ppermute | solution.py:213
  96.1 16.5 %collective-permute-start.9 = (f32[9,4,22,128]{3,2,1,0:T(8,128)S(1)}, f32[9,4,22,128]{3,2,1,0:T(8,128)S(1)}, u32[]{:S(2)}, u32[]{:S(2)}) collective-permute-start(f32[9,4,22,128]{3,2,1,0:T(8,128)S(1)} %fusion.63), channel_id=1, source_target_pairs={{8,16},{16,8},{9,17},{17,9},{10,18},{18,10},{11,19},{19,11},{12,20... | collective-permute-start | bytes 1216520 | tf_op jit(solution)/shard_map/ppermute | solution.py:203
  106.2 6.4 %collective-permute-start.8 = (f32[9,4,22,128]{3,2,1,0:T(8,128)S(1)}, f32[9,4,22,128]{3,2,1,0:T(8,128)S(1)}, u32[]{:S(2)}, u32[]{:S(2)}) collective-permute-start(f32[9,4,22,128]{3,2,1,0:T(8,128)S(1)} %fusion.63), channel_id=1, source_target_pairs={{0,8},{16,24},{8,0},{24,16},{1,9},{17,25},{9,1},{25,17},{2,10},{18... | collective-permute-start | bytes 1216520 | tf_op jit(solution)/shard_map/ppermute | solution.py:204
  116.8 72.4 %copy-start.5 = (f32[1,1,2048]{2,1,0:T(1,128)S(1)}, f32[1,1,2048]{2,1,0:T(1,128)}, u32[]{:S(2)}) copy-start(f32[1,1,2048]{2,1,0:T(1,128)} %param.14) | copy-start | bytes 24580
  189.8 17.0 %all-to-all-start.4 = ((f32[32,8,128]{2,1,0:T(8,128)}), f32[32,8,128]{2,1,0:T(8,128)S(1)}, u32[]{:S(2)}, u32[]{:S(2)}) async-start(f32[32,8,128]{2,1,0:T(8,128)} %shard_map.116), calls=%async_computation.4 | async-start | bytes 262144 | tf_op jit(solution)/shard_map/all_to_all | solution.py:183

commit v4 on v3

--- a/solution.py
+++ b/solution.py
@@ -12,13 +12,26 @@
 STATIC_WEIGHT = 0.6
 F32 = jnp.float32
 BF16 = jnp.bfloat16
-HIGH = lax.Precision.HIGH
 HIGHEST = lax.Precision.HIGHEST
 
 
 def halves(value):
     top = value.astype(BF16)
     return top, (value - top.astype(F32)).astype(BF16)
+
+
+def product(value, weights):
+    top, low = halves(value)
+    w_top, w_low = halves(weights)
+    pair = jnp.concatenate(
+        [
+            jnp.concatenate([w_top, w_low], axis=1),
+            jnp.concatenate([w_top, jnp.zeros_like(w_low)], axis=1),
+        ],
+        axis=0,
+    )
+    both = jnp.dot(jnp.concatenate([top, low], axis=1), pair, preferred_element_type=F32)
+    return both[:, : weights.shape[1]] + both[:, weights.shape[1] :]
 
 
 def one_hot(rows, index):
@@ -48,10 +61,13 @@
     members, slots, cells, levels = anomaly_ref.shape
     at_cell, at_level = observed(slot_ref, index_ref, slots, cells, levels)
     top, low = halves(jnp.where(at_level, first_ref[...] * second_ref[...], 0.0))
-    contract = (((1,), (1,)), ((), ()))
-    grid = lax.dot_general(at_cell, top, contract, preferred_element_type=F32) + lax.dot_general(
-        at_cell, low, contract, preferred_element_type=F32
-    )
+    both = lax.dot_general(
+        at_cell,
+        jnp.concatenate([top, low], axis=0),
+        (((1,), (1,)), ((), ())),
+        preferred_element_type=F32,
+    )
+    grid = both[:, :levels] + both[:, levels:]
     parts = [grid[s * cells : (s + 1) * cells] for s in range(slots)]
     weighted = [ens_weight * part for part in parts]
 
@@ -87,20 +103,15 @@
     cells_x = x_ref.shape[1]
     cells_y = cells // cells_x
     at_cell, at_level = observed(slot_ref, index_ref, slots, cells, levels)
-    contract = (((0,), (0,)), ((), ()))
+    pieces = []
     for which in range(2):
         for x in range(cells_x):
             wide_ref[...] = sum(x_ref[which, x, o] * stack_ref[:, x + o] for o in range(2 * HW + 1))
             held_ref[:, x * cells_y : (x + 1) * cells_y, :] = sum(
                 y_ref[which, o][None] * wide_ref[:, o : o + cells_y, :] for o in range(2 * HW + 1)
             )
-        top, low = halves(held_ref[...].reshape((members + 1) * cells, levels))
-        z_top, z_low = halves(z_ref[which])
-        smooth = (
-            jnp.dot(top, z_top, preferred_element_type=F32)
-            + jnp.dot(top, z_low, preferred_element_type=F32)
-            + jnp.dot(low, z_top, preferred_element_type=F32)
-        ).reshape(members + 1, cells, levels)
+        flat = held_ref[...].reshape((members + 1) * cells, levels)
+        smooth = product(flat, z_ref[which]).reshape(members + 1, cells, levels)
         static = (share * STATIC_WEIGHT) * sigma_ref[...] * smooth[members]
         parts = []
         for s in range(slots):
@@ -109,12 +120,18 @@
         field = jnp.concatenate(parts, axis=0)
         if which == 0:
             field_ref[...] = field
-        top, low = halves(field)
-        columns = lax.dot_general(
-            top, at_cell, contract, preferred_element_type=F32
-        ) + lax.dot_general(low, at_cell, contract, preferred_element_type=F32)
+        pieces.extend(halves(field))
+    columns = lax.dot_general(
+        jnp.concatenate(pieces, axis=1),
+        at_cell,
+        (((0,), (0,)), ((), ())),
+        preferred_element_type=F32,
+    )
+    for which in range(2):
+        first = 2 * which * levels
+        column = columns[first : first + levels] + columns[first + levels : first + 2 * levels]
         value_ref[which : which + 1, :] = jnp.sum(
-            jnp.where(at_level, columns, 0.0), axis=0, keepdims=True
+            jnp.where(at_level, column, 0.0), axis=0, keepdims=True
         )
 
 
@@ -143,7 +160,9 @@
     products_ref[...] = jnp.broadcast_to(jnp.concatenate(sums, axis=0)[None], products_ref.shape)
 
 
-def mix_kernel(products_ref, first_ref, second_ref, total_ref, control_ref, static_ref, field_ref):
+def mix_kernel(
+    products_ref, first_ref, second_ref, z_ref, total_ref, control_ref, static_ref, field_ref
+):
     sums = jnp.sum(jnp.sum(products_ref[...], axis=0), axis=1, keepdims=True)
     p00, p01, p11, p02, p12 = (sums[i : i + 1] for i in range(5))
     step0 = p00 / (p00 + p01)
@@ -156,10 +175,11 @@
     step1 = next_norm / (own + cross)
     mix0 = step0 + step1 * lead
     mix1 = -step1 * step0
-    members = control_ref.shape[0]
-    for i in range(members):
-        control_ref[i] = mix0 * first_ref[i] + mix1 * second_ref[i]
-    static_ref[...] = mix0 * first_ref[members] + mix1 * second_ref[members]
+    members, cells, levels = control_ref.shape
+    mixed = (mix0 * first_ref[...] + mix1 * second_ref[...]).reshape(-1, levels)
+    smooth = product(mixed, z_ref[...])
+    control_ref[...] = smooth[: members * cells].reshape(members, cells, levels)
+    static_ref[...] = smooth[members * cells :]
     near = total_ref.shape[0]
     rows = field_ref.shape[0] // near
     skip = total_ref.shape[1] - 2 * rows
@@ -228,10 +248,8 @@
     return total
 
 
-def flipped(table):
-    rows = table.shape[0]
-    padded = jnp.pad(table, ((HW, HW), (0, 0)))
-    return jnp.stack([padded[o : o + rows, 2 * HW - o] for o in range(2 * HW + 1)], axis=1)
+def flipped(wide, count):
+    return jnp.stack([wide[o : o + count, 2 * HW - o] for o in range(2 * HW + 1)], axis=1)
 
 
 def window(table, axis, count, rim):
@@ -248,14 +266,10 @@
     count = obs_index.shape[-1]
     rows = count // levels
 
-    near = 8 if member_devices % 8 == 0 else 1
+    near = 4 if member_devices % 4 == 0 else 1
     far = member_devices // near
     near_groups = groups(member_devices, near, 1)
     far_groups = groups(member_devices, far, near)
-    close = 4 if member_devices % 4 == 0 else 1
-    wide = member_devices // close
-    close_groups = groups(member_devices, close, 1)
-    wide_groups = groups(member_devices, wide, close)
 
     index = obs_index.reshape(1, -1)
     slot = obs_slot.reshape(1, -1)
@@ -264,15 +278,14 @@
 
     x_rows_wide = window(taper_x, "sx", cells_x, HW)
     x_rows = x_rows_wide[HW : HW + cells_x]
-    x_flip = window(flipped(taper_x), "sx", cells_x, 0)
+    x_flip = flipped(x_rows_wide, cells_x)
     y_rows_wide = window(taper_y, "sy", cells_y, HW)
     y_rows = y_rows_wide[HW : HW + cells_y]
-    y_flip = window(flipped(taper_y), "sy", cells_y, 0)
+    y_flip = flipped(y_rows_wide, cells_y)
     x_pair = jnp.stack([x_rows, x_flip])
     y_pair = jnp.broadcast_to(
         jnp.stack([y_rows.T, y_flip.T])[..., None], (2, 2 * HW + 1, cells_y, levels)
     )
-    z_pair = jnp.stack([taper_z, taper_z.T])
 
     params = pltpu.CompilerParams(vmem_limit_bytes=40 * 2**20)
     packed = anomalies.reshape(local_members, slots, cells, levels)
@@ -280,7 +293,15 @@
     side = cells_x * 2 * HW
     wide_y = cells_y + 2 * HW
 
-    def apply(first, second, room):
+    whole = pl.BlockSpec(memory_space=pltpu.VMEM)
+
+    def z_products(after):
+        table, after = lax.optimization_barrier((taper_z, after))
+        return jnp.stack(
+            [jnp.dot(table, other, precision=HIGHEST) for other in (table, table.T)]
+        ), after
+
+    def apply(first, second, room, z_pair=None):
         stack, low, high = pl.pallas_call(
             functools.partial(adjoint_kernel, ens_weight, cells_y),
             out_shape=(
@@ -295,10 +316,10 @@
             block.reshape(local_members + 1, cells_x, -1, levels) for block in (left, stack, right)
         ]
         stack = taps(jnp.concatenate(pieces, axis=2), y_rows_wide, 2, wide_y)
+        if z_pair is None:
+            z_pair, stack = z_products(stack)
         stack = taps(widened(stack, 2 * HW - cells_x, "sx"), x_rows_wide, 1, cells_x + 2 * HW)
-        stack = jnp.einsum("bxyk,kl->bxyl", stack, taper_z, precision=HIGH)
         control = stack[:, HW : HW + cells_x, HW : HW + cells_y]
-        whole = pl.BlockSpec(memory_space=pltpu.VMEM)
         field, sampled = pl.pallas_call(
             functools.partial(forward_kernel, ens_weight, share),
             out_shape=(
@@ -312,17 +333,17 @@
             ],
             compiler_params=params,
         )(x_pair, slot, index, stack, y_pair, z_pair, packed, packed_sigma)
-        return control, field, sampled.reshape(2, rows, levels)
-
-    control0, field0, sampled0 = apply(obs_weight, first, 60)
-    part = jnp.sum(gathered(sampled0[0], close, "member", close_groups), axis=0)
-    seen0 = lax.psum(part, "member", axis_index_groups=wide_groups)
-    control1, field1, sampled1 = apply(obs_weight, seen0.reshape(1, -1), 40)
+        return control, field, sampled.reshape(2, rows, levels), z_pair
+
+    control0, field0, sampled0, z_pair = apply(obs_weight, first, 60)
+    part = jnp.sum(gathered(sampled0[0], near, "member", near_groups), axis=0)
+    seen0 = lax.psum(part, "member", axis_index_groups=far_groups)
+    control1, field1, sampled1, _ = apply(obs_weight, seen0.reshape(1, -1), 40, z_pair)
 
     blocks = (sampled0[1], sampled1[0], sampled1[1], field0, field1)
     flat = jnp.concatenate([block.reshape(near, -1, levels) for block in blocks], axis=1)
     chunk = jnp.sum(exchange(flat, "member", near_groups), axis=0)
-    chunk = jnp.sum(gathered(chunk, far, "member", far_groups), axis=0)
+    chunk = lax.psum(chunk, "member", axis_index_groups=far_groups)
     total = gathered(chunk, near, "member", near_groups)
     regions = lax.axis_size("sx") * lax.axis_size("sy")
     products = pl.pallas_call(
@@ -343,6 +364,7 @@
         products,
         control0.reshape(-1, cells, levels),
         control1.reshape(-1, cells, levels),
+        taper_z,
         total,
     )
     shape = (cells_x, cells_y, levels)

time: 209 us -> 194 us (0.928)
  blocking collectives: 107 us -> 87.7 us
  starting transfers between devices: 53.5 us -> 59.2 us
    all_to_all x4 -> x3, blocking collectives: 78.8 us -> 23.7 us  [exchange(): lax.all_to_all(blocks, axis, 0, 0, axis_index_groups=index_groups, tiled=...]
    psum x1 -> x2, blocking collectives: 28.1 us -> 64 us  [the longest x1 36 us: body(): chunk = lax.psum(chunk, 'member', axis_index_groups=far_groups)]
    all_to_all x1, starting transfers between devices: 9.28 us -> 14.4 us  [exchange(): lax.all_to_all(blocks, axis, 0, 0, axis_index_groups=index_groups, tiled=...]
  transfers between devices with their start and end apart: 11 -> 11, of which waited for: 6 -> 6; matrix products, arithmetic and copies ran while one was open for 2% -> 1% of each run, Pallas kernels for 0% -> 0%
where the time goes in v4:
time: 194 us; the launch traced here: 193 us
  blocking collectives  87.7 us (45%)
  starting transfers between devices  59.2 us (31%)
  waiting for transfers between devices  28.3 us (15%)
  Pallas kernels  10.1 us (5%)
  other arithmetic  3.6 us (2%)
  local copies, waits for them, and re-layouts  2.99 us (2%)
    psum x1, blocking collectives, body(): chunk = lax.psum(chunk, 'member', axis_index_groups=far_groups)  36 us
    psum x1, blocking collectives, body(): seen0 = lax.psum(part, 'member', axis_index_groups=far_groups)  28.1 us
    all_to_all x3, blocking collectives, exchange(): lax.all_to_all(blocks, axis, 0, 0, axis_index_groups=index_groups, tiled=...  23.7 us
    ppermute x2, starting transfers between devices, paired(): lax.ppermute(jnp.where(upper, high_side, low_side), axis, odd + [(j, i) f...  15.7 us
    all_to_all x1, starting transfers between devices, exchange(): lax.all_to_all(blocks, axis, 0, 0, axis_index_groups=index_groups, tiled=...  14.4 us
    ppermute x2, starting transfers between devices, paired(): lax.ppermute(jnp.where(upper, low_side, high_side), axis, even + [(j, i)...  11.3 us
    ppermute x2, starting transfers between devices, neighbours(): lax.ppermute(high_side, axis, up)  11.1 us
    ppermute x2, waiting for transfers between devices, neighbours(): lax.ppermute(low_side, axis, down)  9.01 us
  transfers between devices with their start and end apart: 11, of which 6 were waited for; matrix products, arithmetic and copies ran while one was open for 1% of the time, Pallas kernels for 0%

profile of v4, /device:TPU:1, one launch (start us, length us, event | category | flops | bytes accessed | tf_op | source)
XLA Modules:
  0.0 193.5 jit_solution(18396272668608391325)
XLA Ops:
  0.6 2.5 %shard_map.112 = (f32[9,64,128]{2,1,0:T(8,128)}, f32[9,24,128]{2,1,0:T(8,128)}, f32[9,24,128]{2,1,0:T(8,128)}) custom-call(s32[1,2048]{1,0:T(1,128)} %bitcast.79, s32[1,2048]{1,0:T(1,128)} %bitcast.83, f32[1,2048]{1,0:T(1,128)} %bitcast.89, f32[1,2048]{1,0:T(1,128)} %bitcast.93, bf16[8,3,64,128]{3,2,1,0:T(8,128)(2,1)} %bitcast.67, f32[64,128]{1,0:T(8,128)} %bitcast.75), custom_call_target="tpu_custom_call" | custom-call | tf_op jit(solution)/shard_map/pallas_call | solution.py:305
  3.1 5.8 %collective-permute-start = (f32[9,24,128]{2,1,0:T(8,128)}, f32[9,24,128]{2,1,0:T(8,128)S(1)}, u32[]{:S(2)}, u32[]{:S(2)}) collective-permute-start(f32[9,24,128]{2,1,0:T(8,128)} %get-tuple-element.18), channel_id=1, source_target_pairs={{0,1},{1,2},{2,3},{3,4},{4,5},{5,6},{6,7},{8,9},{9,10},{10,11},{11... | collective-permute-start | bytes 331784 | tf_op jit(solution)/shard_map/ppermute | solution.py:214
  8.9 1.3 collective-permute-start.1
  10.2 0.8 pad_dynamic-slice_fusion
  11.0 0.1 fusion.30
  11.1 0.1 slice_bitcast_fusion
  11.1 0.8 pad_dynamic-slice_fusion.1
  11.9 0.1 fusion.31
  12.0 0.1 copy.16
  12.2 0.1 copy.17
  12.3 3.8 %collective-permute-done.1 = f32[9,24,128]{2,1,0:T(8,128)S(1)} collective-permute-done((f32[9,24,128]{2,1,0:T(8,128)}, f32[9,24,128]{2,1,0:T(8,128)S(1)}, u32[]{:S(2)}, u32[]{:S(2)}) %collective-permute-start.1) | collective-permute-done | bytes 110624 | tf_op jit(solution)/shard_map/ppermute | solution.py:214
  16.1 1.0 pad_maximum_fusion.14
  17.2 0.4 fusion.23
  17.6 4.3 %collective-permute-start.4 = (f32[9,4,22,128]{3,2,1,0:T(8,128)S(1)}, f32[9,4,22,128]{3,2,1,0:T(8,128)S(1)}, u32[]{:S(2)}, u32[]{:S(2)}) collective-permute-start(f32[9,4,22,128]{3,2,1,0:T(8,128)S(1)} %fusion.23), channel_id=1, source_target_pairs={{8,16},{16,8},{9,17},{17,9},{10,18},{18,10},{11,19},{19,11},{12,20... | collective-permute-start | bytes 1216520 | tf_op jit(solution)/shard_map/ppermute | solution.py:223
  21.9 9.4 %collective-permute-start.3 = (f32[9,4,22,128]{3,2,1,0:T(8,128)S(1)}, f32[9,4,22,128]{3,2,1,0:T(8,128)S(1)}, u32[]{:S(2)}, u32[]{:S(2)}) collective-permute-start(f32[9,4,22,128]{3,2,1,0:T(8,128)S(1)} %fusion.23), channel_id=1, source_target_pairs={{0,8},{16,24},{8,0},{24,16},{1,9},{17,25},{9,1},{25,17},{2,10},{18... | collective-permute-start | bytes 1216520 | tf_op jit(solution)/shard_map/ppermute | solution.py:224
  31.3 0.3 convolution_bitcast_fusion
  31.6 1.9 collective-permute-start.2
  33.5 0.2 convolution_bitcast_fusion.1
  33.8 6.8 %collective-permute-done.2 = f32[9,2,22,128]{3,2,1,0:T(8,128)S(1)} collective-permute-done((f32[9,2,22,128]{3,2,1,0:T(8,128)S(1)}, f32[9,2,22,128]{3,2,1,0:T(8,128)S(1)}, u32[]{:S(2)}, u32[]{:S(2)}) %collective-permute-start.2) | collective-permute-done | bytes 202784 | tf_op jit(solution)/shard_map/ppermute | solution.py:233
  40.7 0.1 pad_maximum_fusion
  40.8 0.6 fusion.10.stack_ref
  41.5 0.1 broadcast_in_dim.8.y_ref
  41.5 0.2 copy-done
  41.8 2.5 %shard_map.113 = (f32[192,128]{1,0:T(8,128)S(1)}, f32[2,2048]{1,0:T(2,128)S(1)}) custom-call(f32[2,4,7]{2,1,0:T(4,128)S(1)} %pad_maximum_fusion.18.x_ref, s32[1,2048]{1,0:T(1,128)S(1)} %bitcast.80, s32[1,2048]{1,0:T(1,128)S(1)} %bitcast.84, f32[9,10,22,128]{3,2,1,0:T(8,128)S(1)} %fusion.10.stack_ref, f32[2,7,16,128]{3,2,1,0:T(8,128)S(1)} %broadcast_in_dim.8.y_ref, ...), custom_call_target="tpu_custom_call" | custom-call | tf_op jit(solution)/shard_map/pallas_call | solution.py:323
  44.4 6.9 %all_to_all.20 = f32[4,16,128]{2,1,0:T(8,128)S(1)} all-to-all(f32[4,16,128]{2,1,0:T(8,128)S(1)} %broadcast_in_dim.10), channel_id=1, replica_groups={{0,32,64,96},{128,160,192,224},{256,288,320,352},{384,416,448,480},{512..., dimensions={0} | all-to-all | bytes 65536 | tf_op jit(solution)/shard_map/all_to_all | solution.py:203
  51.2 28.1 %psum.14.seen_ref = f32[16,128]{1,0:T(8,128)S(1)} all-reduce(f32[16,128]{1,0:T(8,128)S(1)} %reduce_sum.18), channel_id=1, replica_groups={{0,128,256,384,512,640,768,896},{32,160,288,416,544,672,800,928},{64,19..., use_global_device_ids=true, to_apply=%region_1.2 | all-reduce | flops 2048 | bytes 16384 | tf_op jit(solution)/shard_map/psum | solution.py:340
  79.3 0.6 shard_map.114
  80.0 5.3 %collective-permute-start.5 = (f32[9,24,128]{2,1,0:T(8,128)S(1)}, f32[9,24,128]{2,1,0:T(8,128)S(1)}, u32[]{:S(2)}, u32[]{:S(2)}) collective-permute-start(f32[9,24,128]{2,1,0:T(8,128)S(1)} %get-tuple-element.24), channel_id=1, source_target_pairs={{0,1},{1,2},{2,3},{3,4},{4,5},{5,6},{6,7},{8,9},{9,10},{10,11},{11... | collective-permute-start | bytes 331784 | tf_op jit(solution)/shard_map/ppermute | solution.py:214
  85.3 1.3 collective-permute-start.6
  86.6 0.4 collective-permute-done.5
  87.0 5.2 %collective-permute-done.6 = f32[9,24,128]{2,1,0:T(8,128)S(1)} collective-permute-done((f32[9,24,128]{2,1,0:T(8,128)S(1)}, f32[9,24,128]{2,1,0:T(8,128)S(1)}, u32[]{:S(2)}, u32[]{:S(2)}) %collective-permute-start.6) | collective-permute-done | bytes 110624 | tf_op jit(solution)/shard_map/ppermute | solution.py:214
  92.3 0.1 pad_maximum_fusion.15
  92.4 0.4 fusion.17
  92.8 2.3 %collective-permute-start.7 = (f32[9,2,22,128]{3,2,1,0:T(8,128)S(1)}, f32[9,2,22,128]{3,2,1,0:T(8,128)S(1)}, u32[]{:S(2)}, u32[]{:S(2)}) collective-permute-start(f32[9,2,22,128]{3,2,1,0:T(8,128)S(1)} %slice_select_fusion), channel_id=1, source_target_pairs={{0,16},{16,0},{8,24},{24,8},{1,17},{17,1},{9,25},{25,9},{2,18},{18... | collective-permute-start | bytes 608264 | tf_op jit(solution)/shard_map/ppermute | solution.py:233
  95.1 11.5 %collective-permute-start.9 = (f32[9,4,22,128]{3,2,1,0:T(8,128)S(1)}, f32[9,4,22,128]{3,2,1,0:T(8,128)S(1)}, u32[]{:S(2)}, u32[]{:S(2)}) collective-permute-start(f32[9,4,22,128]{3,2,1,0:T(8,128)S(1)} %fusion.17), channel_id=1, source_target_pairs={{8,16},{16,8},{9,17},{17,9},{10,18},{18,10},{11,19},{19,11},{12,20... | collective-permute-start | bytes 1216520 | tf_op jit(solution)/shard_map/ppermute | solution.py:223
  106.5 1.9 collective-permute-start.8
  108.5 4.4 %collective-permute-done.9 = f32[9,4,22,128]{3,2,1,0:T(8,128)S(1)} collective-permute-done((f32[9,4,22,128]{3,2,1,0:T(8,128)S(1)}, f32[9,4,22,128]{3,2,1,0:T(8,128)S(1)}, u32[]{:S(2)}, u32[]{:S(2)}) %collective-permute-start.9) | collective-permute-done | bytes 405536 | tf_op jit(solution)/shard_map/ppermute | solution.py:223
  113.0 0.1 pad_maximum_fusion.1
  113.1 0.6 fusion.2.stack_ref
  113.7 2.6 %shard_map.115 = (f32[192,128]{1,0:T(8,128)S(1)}, f32[2,2048]{1,0:T(2,128)S(1)}) custom-call(f32[2,4,7]{2,1,0:T(4,128)S(1)} %pad_maximum_fusion.18.x_ref, s32[1,2048]{1,0:T(1,128)S(1)} %bitcast.82, s32[1,2048]{1,0:T(1,128)S(1)} %bitcast.86, f32[9,10,22,128]{3,2,1,0:T(8,128)S(1)} %fusion.2.stack_ref, f32[2,7,16,128]{3,2,1,0:T(8,128)S(1)} %broadcast_in_dim.8.y_ref, ...), custom_call_target="tpu_custom_call" | custom-call | tf_op jit(solution)/shard_map/pallas_call | solution.py:323
  116.4 0.4 concatenate.73
  116.7 8.7 %all_to_all.21 = f32[4,108,128]{2,1,0:T(8,128)S(1)} all-to-all(f32[4,108,128]{2,1,0:T(8,128)S(1)} %concatenate.73), channel_id=1, replica_groups={{0,32,64,96},{128,160,192,224},{256,288,320,352},{384,416,448,480},{512..., dimensions={0} | all-to-all | bytes 442368 | tf_op jit(solution)/shard_map/all_to_all | solution.py:203
  125.5 36.0 %psum.15 = f32[108,128]{1,0:T(8,128)S(1)} all-reduce(f32[108,128]{1,0:T(8,128)S(1)} %reduce_sum.19), channel_id=1, replica_groups={{0,128,256,384,512,640,768,896},{32,160,288,416,544,672,800,928},{64,19..., use_global_device_ids=true, to_apply=%region_3.4 | all-reduce | flops 13824 | bytes 110592 | tf_op jit(solution)/shard_map/psum | solution.py:346
  161.4 8.1 %all_to_all.22.total_ref = f32[4,108,128]{2,1,0:T(8,128)S(1)} all-to-all(f32[4,108,128]{2,1,0:T(8,128)S(1)} %broadcast_in_dim.22), channel_id=1, replica_groups={{0,32,64,96},{128,160,192,224},{256,288,320,352},{384,416,448,480},{512..., dimensions={0} | all-to-all | bytes 442368 | tf_op jit(solution)/shard_map/all_to_all | solution.py:203
  169.6 0.7 shard_map.116
  170.2 14.4 %all-to-all-start.3 = ((f32[32,8,128]{2,1,0:T(8,128)}), f32[32,8,128]{2,1,0:T(8,128)S(1)}, u32[]{:S(2)}, u32[]{:S(2)}) async-start(f32[32,8,128]{2,1,0:T(8,128)} %shard_map.116), calls=%async_computation.3 | async-start | bytes 262144 | tf_op jit(solution)/shard_map/all_to_all | solution.py:203
  184.7 7.7 %all-to-all-done.3.products_ref = f32[32,8,128]{2,1,0:T(8,128)S(1)} async-done(((f32[32,8,128]{2,1,0:T(8,128)}), f32[32,8,128]{2,1,0:T(8,128)S(1)}, u32[]{:S(2)}, u32[]{:S(2)}) %all-to-all-start.3) | async-done | bytes 131104 | tf_op jit(solution)/shard_map/all_to_all | solution.py:203
  192.4 1.1 shard_map.117
  (46 shorter events, 0.6 us)
Async XLA Ops:
  3.1 14.1 %copy-start.7 = (f32[9,64,128]{2,1,0:T(8,128)S(1)}, f32[9,64,128]{2,1,0:T(8,128)}, u32[]{:S(2)}) copy-start(f32[9,64,128]{2,1,0:T(8,128)} %get-tuple-element.19) | copy-start | bytes 884740
  3.1 9.2 %collective-permute-start = (f32[9,24,128]{2,1,0:T(8,128)}, f32[9,24,128]{2,1,0:T(8,128)S(1)}, u32[]{:S(2)}, u32[]{:S(2)}) collective-permute-start(f32[9,24,128]{2,1,0:T(8,128)} %get-tuple-element.18), channel_id=1, source_target_pairs={{0,1},{1,2},{2,3},{3,4},{4,5},{5,6},{6,7},{8,9},{9,10},{10,11},{11... | collective-permute-start | bytes 331784 | tf_op jit(solution)/shard_map/ppermute | solution.py:214
  8.9 7.2 %collective-permute-start.1 = (f32[9,24,128]{2,1,0:T(8,128)}, f32[9,24,128]{2,1,0:T(8,128)S(1)}, u32[]{:S(2)}, u32[]{:S(2)}) collective-permute-start(f32[9,24,128]{2,1,0:T(8,128)} %get-tuple-element.20), channel_id=1, source_target_pairs={{1,0},{2,1},{3,2},{4,3},{5,4},{6,5},{7,6},{9,8},{10,9},{11,10},{12... | collective-permute-start | bytes 331784 | tf_op jit(solution)/shard_map/ppermute | solution.py:214
  17.2 14.1 %copy-start.1 = (f32[128,128]{1,0:T(8,128)S(1)}, f32[128,128]{1,0:T(8,128)}, u32[]{:S(2)}) copy-start(f32[128,128]{1,0:T(8,128)} %z_ref.1) | copy-start | bytes 196612
  17.6 23.0 %collective-permute-start.4 = (f32[9,4,22,128]{3,2,1,0:T(8,128)S(1)}, f32[9,4,22,128]{3,2,1,0:T(8,128)S(1)}, u32[]{:S(2)}, u32[]{:S(2)}) collective-permute-start(f32[9,4,22,128]{3,2,1,0:T(8,128)S(1)} %fusion.23), channel_id=1, source_target_pairs={{8,16},{16,8},{9,17},{17,9},{10,18},{18,10},{11,19},{19,11},{12,20... | collective-permute-start | bytes 1216520 | tf_op jit(solution)/shard_map/ppermute | solution.py:223
  21.9 18.7 %collective-permute-start.3 = (f32[9,4,22,128]{3,2,1,0:T(8,128)S(1)}, f32[9,4,22,128]{3,2,1,0:T(8,128)S(1)}, u32[]{:S(2)}, u32[]{:S(2)}) collective-permute-start(f32[9,4,22,128]{3,2,1,0:T(8,128)S(1)} %fusion.23), channel_id=1, source_target_pairs={{0,8},{16,24},{8,0},{24,16},{1,9},{17,25},{9,1},{25,17},{2,10},{18... | collective-permute-start | bytes 1216520 | tf_op jit(solution)/shard_map/ppermute | solution.py:224
  31.6 8.9 %collective-permute-start.2 = (f32[9,2,22,128]{3,2,1,0:T(8,128)S(1)}, f32[9,2,22,128]{3,2,1,0:T(8,128)S(1)}, u32[]{:S(2)}, u32[]{:S(2)}) collective-permute-start(f32[9,2,22,128]{3,2,1,0:T(8,128)S(1)} %slice_select_fusion.1), channel_id=1, source_target_pairs={{0,16},{16,0},{8,24},{24,8},{1,17},{17,1},{9,25},{25,9},{2,18},{18... | collective-permute-start | bytes 608264 | tf_op jit(solution)/shard_map/ppermute | solution.py:233
  40.8 1.0 copy-start
  40.8 1.0 copy-start.2
  40.8 1.0 copy-start.3
  40.8 1.0 copy-start.4
  41.4 37.9 %copy-start.5 = (f32[1,1,2048]{2,1,0:T(1,128)S(1)}, f32[1,1,2048]{2,1,0:T(1,128)}, u32[]{:S(2)}) copy-start(f32[1,1,2048]{2,1,0:T(1,128)} %param.15) | copy-start | bytes 24580
  80.0 7.0 %collective-permute-start.5 = (f32[9,24,128]{2,1,0:T(8,128)S(1)}, f32[9,24,128]{2,1,0:T(8,128)S(1)}, u32[]{:S(2)}, u32[]{:S(2)}) collective-permute-start(f32[9,24,128]{2,1,0:T(8,128)S(1)} %get-tuple-element.24), channel_id=1, source_target_pairs={{0,1},{1,2},{2,3},{3,4},{4,5},{5,6},{6,7},{8,9},{9,10},{10,11},{11... | collective-permute-start | bytes 331784 | tf_op jit(solution)/shard_map/ppermute | solution.py:214
  85.3 7.0 %collective-permute-start.6 = (f32[9,24,128]{2,1,0:T(8,128)S(1)}, f32[9,24,128]{2,1,0:T(8,128)S(1)}, u32[]{:S(2)}, u32[]{:S(2)}) collective-permute-start(f32[9,24,128]{2,1,0:T(8,128)S(1)} %get-tuple-element.26), channel_id=1, source_target_pairs={{1,0},{2,1},{3,2},{4,3},{5,4},{6,5},{7,6},{9,8},{10,9},{11,10},{12... | collective-permute-start | bytes 331784 | tf_op jit(solution)/shard_map/ppermute | solution.py:214
  92.8 15.7 %collective-permute-start.7 = (f32[9,2,22,128]{3,2,1,0:T(8,128)S(1)}, f32[9,2,22,128]{3,2,1,0:T(8,128)S(1)}, u32[]{:S(2)}, u32[]{:S(2)}) collective-permute-start(f32[9,2,22,128]{3,2,1,0:T(8,128)S(1)} %slice_select_fusion), channel_id=1, source_target_pairs={{0,16},{16,0},{8,24},{24,8},{1,17},{17,1},{9,25},{25,9},{2,18},{18... | collective-permute-start | bytes 608264 | tf_op jit(solution)/shard_map/ppermute | solution.py:233
  95.1 17.9 %collective-permute-start.9 = (f32[9,4,22,128]{3,2,1,0:T(8,128)S(1)}, f32[9,4,22,128]{3,2,1,0:T(8,128)S(1)}, u32[]{:S(2)}, u32[]{:S(2)}) collective-permute-start(f32[9,4,22,128]{3,2,1,0:T(8,128)S(1)} %fusion.17), channel_id=1, source_target_pairs={{8,16},{16,8},{9,17},{17,9},{10,18},{18,10},{11,19},{19,11},{12,20... | collective-permute-start | bytes 1216520 | tf_op jit(solution)/shard_map/ppermute | solution.py:223
  106.5 6.4 %collective-permute-start.8 = (f32[9,4,22,128]{3,2,1,0:T(8,128)S(1)}, f32[9,4,22,128]{3,2,1,0:T(8,128)S(1)}, u32[]{:S(2)}, u32[]{:S(2)}) collective-permute-start(f32[9,4,22,128]{3,2,1,0:T(8,128)S(1)} %fusion.17), channel_id=1, source_target_pairs={{0,8},{16,24},{8,0},{24,16},{1,9},{17,25},{9,1},{25,17},{2,10},{18... | collective-permute-start | bytes 1216520 | tf_op jit(solution)/shard_map/ppermute | solution.py:224
  116.3 53.2 %copy-start.6 = (f32[1,1,2048]{2,1,0:T(1,128)S(1)}, f32[1,1,2048]{2,1,0:T(1,128)}, u32[]{:S(2)}) copy-start(f32[1,1,2048]{2,1,0:T(1,128)} %param.14) | copy-start | bytes 24580
  170.2 22.1 %all-to-all-start.3 = ((f32[32,8,128]{2,1,0:T(8,128)}), f32[32,8,128]{2,1,0:T(8,128)S(1)}, u32[]{:S(2)}, u32[]{:S(2)}) async-start(f32[32,8,128]{2,1,0:T(8,128)} %shard_map.116), calls=%async_computation.3 | async-start | bytes 262144 | tf_op jit(solution)/shard_map/all_to_all | solution.py:203

commit v5 on v4

--- a/solution.py
+++ b/solution.py
@@ -155,16 +155,19 @@
         (weight2, flip0),
         (weight2, flip1),
     )
-    sums = [jnp.sum(a * b, axis=0, keepdims=True) for a, b in pairs]
-    sums.append(jnp.zeros((products_ref.shape[1] - len(pairs), levels), F32))
-    products_ref[...] = jnp.broadcast_to(jnp.concatenate(sums, axis=0)[None], products_ref.shape)
+    lane = lax.broadcasted_iota(jnp.int32, (1, levels), 1)
+    line = jnp.zeros((1, levels), F32)
+    for i, (a, b) in enumerate(pairs):
+        column = jnp.sum(a * b, axis=0, keepdims=True)
+        line = jnp.where(lane == i, jnp.sum(column, axis=1, keepdims=True), line)
+    products_ref[...] = jnp.broadcast_to(line, products_ref.shape)
 
 
 def mix_kernel(
     products_ref, first_ref, second_ref, z_ref, total_ref, control_ref, static_ref, field_ref
 ):
-    sums = jnp.sum(jnp.sum(products_ref[...], axis=0), axis=1, keepdims=True)
-    p00, p01, p11, p02, p12 = (sums[i : i + 1] for i in range(5))
+    sums = jnp.sum(products_ref[...], axis=0, keepdims=True)
+    p00, p01, p11, p02, p12 = (sums[:, i : i + 1] for i in range(5))
     step0 = p00 / (p00 + p01)
     keep = 1.0 - step0
     next_norm = keep * (keep * p00 - 2.0 * step0 * p01) + step0 * step0 * p11
@@ -348,7 +351,7 @@
     regions = lax.axis_size("sx") * lax.axis_size("sy")
     products = pl.pallas_call(
         product_kernel,
-        out_shape=jax.ShapeDtypeStruct((regions, 8, levels), F32),
+        out_shape=jax.ShapeDtypeStruct((regions, levels), F32),
         compiler_params=params,
     )(total, obs_inverse.reshape(rows, levels), innovation.reshape(rows, levels), seen0)
     products = exchange(products, ("sx", "sy"))

time: 194 us -> 193 us (level)
  no operation moved by 1% of the time
where the time goes in v5:
time: 193 us
  blocking collectives  87.7 us (45%)
  starting transfers between devices  59.2 us (31%)
  waiting for transfers between devices  27.5 us (14%)
  Pallas kernels  10.1 us (5%)
  other arithmetic  3.6 us (2%)
  local copies, waits for them, and re-layouts  2.99 us (2%)
    psum x1, blocking collectives, body(): chunk = lax.psum(chunk, 'member', axis_index_groups=far_groups)  36 us
    psum x1, blocking collectives, body(): seen0 = lax.psum(part, 'member', axis_index_groups=far_groups)  28.1 us
    all_to_all x3, blocking collectives, exchange(): lax.all_to_all(blocks, axis, 0, 0, axis_index_groups=index_groups, tiled=...  23.7 us
    ppermute x2, starting transfers between devices, paired(): lax.ppermute(jnp.where(upper, high_side, low_side), axis, odd + [(j, i) f...  15.7 us
    all_to_all x1, starting transfers between devices, exchange(): lax.all_to_all(blocks, axis, 0, 0, axis_index_groups=index_groups, tiled=...  14.4 us
    ppermute x2, starting transfers between devices, paired(): lax.ppermute(jnp.where(upper, low_side, high_side), axis, even + [(j, i)...  11.3 us
    ppermute x2, starting transfers between devices, neighbours(): lax.ppermute(high_side, axis, up)  11.1 us
    ppermute x2, waiting for transfers between devices, neighbours(): lax.ppermute(low_side, axis, down)  9.01 us
  transfers between devices with their start and end apart: 11, of which 6 were waited for; matrix products, arithmetic and copies ran while one was open for 1% of the time, Pallas kernels for 0%

profile of v5, /device:TPU:1, one launch (start us, length us, event | category | flops | bytes accessed | tf_op | source)
XLA Modules:
  0.0 192.6 jit_solution(15231766826325054388)
XLA Ops:
  0.6 2.5 %shard_map.112 = (f32[9,64,128]{2,1,0:T(8,128)}, f32[9,24,128]{2,1,0:T(8,128)}, f32[9,24,128]{2,1,0:T(8,128)}) custom-call(s32[1,2048]{1,0:T(1,128)} %bitcast.83, s32[1,2048]{1,0:T(1,128)} %bitcast.87, f32[1,2048]{1,0:T(1,128)} %bitcast.93, f32[1,2048]{1,0:T(1,128)} %bitcast.98, bf16[8,3,64,128]{3,2,1,0:T(8,128)(2,1)} %bitcast.71, f32[64,128]{1,0:T(8,128)} %bitcast.79), custom_call_target="tpu_custom_call" | custom-call | tf_op jit(solution)/shard_map/pallas_call | solution.py:308
  3.1 5.8 %collective-permute-start = (f32[9,24,128]{2,1,0:T(8,128)}, f32[9,24,128]{2,1,0:T(8,128)S(1)}, u32[]{:S(2)}, u32[]{:S(2)}) collective-permute-start(f32[9,24,128]{2,1,0:T(8,128)} %get-tuple-element.18), channel_id=1, source_target_pairs={{0,1},{1,2},{2,3},{3,4},{4,5},{5,6},{6,7},{8,9},{9,10},{10,11},{11... | collective-permute-start | bytes 331784 | tf_op jit(solution)/shard_map/ppermute | solution.py:217
  8.9 1.3 collective-permute-start.1
  10.2 0.8 pad_dynamic-slice_fusion
  11.0 0.1 fusion.30
  11.1 0.1 slice_bitcast_fusion
  11.1 0.8 pad_dynamic-slice_fusion.1
  11.9 0.1 fusion.31
  12.0 0.1 copy.19
  12.2 0.1 copy.20
  12.3 3.8 %collective-permute-done.1 = f32[9,24,128]{2,1,0:T(8,128)S(1)} collective-permute-done((f32[9,24,128]{2,1,0:T(8,128)}, f32[9,24,128]{2,1,0:T(8,128)S(1)}, u32[]{:S(2)}, u32[]{:S(2)}) %collective-permute-start.1) | collective-permute-done | bytes 110624 | tf_op jit(solution)/shard_map/ppermute | solution.py:217
  16.1 1.0 pad_maximum_fusion.14
  17.2 0.4 fusion.23
  17.6 4.3 %collective-permute-start.4 = (f32[9,4,22,128]{3,2,1,0:T(8,128)S(1)}, f32[9,4,22,128]{3,2,1,0:T(8,128)S(1)}, u32[]{:S(2)}, u32[]{:S(2)}) collective-permute-start(f32[9,4,22,128]{3,2,1,0:T(8,128)S(1)} %fusion.23), channel_id=1, source_target_pairs={{8,16},{16,8},{9,17},{17,9},{10,18},{18,10},{11,19},{19,11},{12,20... | collective-permute-start | bytes 1216520 | tf_op jit(solution)/shard_map/ppermute | solution.py:226
  21.9 9.4 %collective-permute-start.3 = (f32[9,4,22,128]{3,2,1,0:T(8,128)S(1)}, f32[9,4,22,128]{3,2,1,0:T(8,128)S(1)}, u32[]{:S(2)}, u32[]{:S(2)}) collective-permute-start(f32[9,4,22,128]{3,2,1,0:T(8,128)S(1)} %fusion.23), channel_id=1, source_target_pairs={{0,8},{16,24},{8,0},{24,16},{1,9},{17,25},{9,1},{25,17},{2,10},{18... | collective-permute-start | bytes 1216520 | tf_op jit(solution)/shard_map/ppermute | solution.py:227
  31.3 0.3 convolution_bitcast_fusion
  31.6 1.9 collective-permute-start.2
  33.5 0.2 convolution_bitcast_fusion.1
  33.8 6.8 %collective-permute-done.2 = f32[9,2,22,128]{3,2,1,0:T(8,128)S(1)} collective-permute-done((f32[9,2,22,128]{3,2,1,0:T(8,128)S(1)}, f32[9,2,22,128]{3,2,1,0:T(8,128)S(1)}, u32[]{:S(2)}, u32[]{:S(2)}) %collective-permute-start.2) | collective-permute-done | bytes 202784 | tf_op jit(solution)/shard_map/ppermute | solution.py:236
  40.7 0.1 pad_maximum_fusion
  40.8 0.6 fusion.10.stack_ref
  41.5 0.1 broadcast_in_dim.8.y_ref
  41.5 0.2 copy-done
  41.8 2.5 %shard_map.113 = (f32[192,128]{1,0:T(8,128)S(1)}, f32[2,2048]{1,0:T(2,128)S(1)}) custom-call(f32[2,4,7]{2,1,0:T(4,128)S(1)} %pad_maximum_fusion.18.x_ref, s32[1,2048]{1,0:T(1,128)S(1)} %bitcast.84, s32[1,2048]{1,0:T(1,128)S(1)} %bitcast.88, f32[9,10,22,128]{3,2,1,0:T(8,128)S(1)} %fusion.10.stack_ref, f32[2,7,16,128]{3,2,1,0:T(8,128)S(1)} %broadcast_in_dim.8.y_ref, ...), custom_call_target="tpu_custom_call" | custom-call | tf_op jit(solution)/shard_map/pallas_call | solution.py:326
  44.4 6.9 %all_to_all.26 = f32[4,16,128]{2,1,0:T(8,128)S(1)} all-to-all(f32[4,16,128]{2,1,0:T(8,128)S(1)} %broadcast_in_dim.10), channel_id=1, replica_groups={{0,32,64,96},{128,160,192,224},{256,288,320,352},{384,416,448,480},{512..., dimensions={0} | all-to-all | bytes 65536 | tf_op jit(solution)/shard_map/all_to_all | solution.py:206
  51.2 28.1 %psum.14.seen_ref = f32[16,128]{1,0:T(8,128)S(1)} all-reduce(f32[16,128]{1,0:T(8,128)S(1)} %reduce_sum.18), channel_id=1, replica_groups={{0,128,256,384,512,640,768,896},{32,160,288,416,544,672,800,928},{64,19..., use_global_device_ids=true, to_apply=%region_1.2 | all-reduce | flops 2048 | bytes 16384 | tf_op jit(solution)/shard_map/psum | solution.py:343
  79.3 0.6 shard_map.114
  80.0 5.3 %collective-permute-start.5 = (f32[9,24,128]{2,1,0:T(8,128)S(1)}, f32[9,24,128]{2,1,0:T(8,128)S(1)}, u32[]{:S(2)}, u32[]{:S(2)}) collective-permute-start(f32[9,24,128]{2,1,0:T(8,128)S(1)} %get-tuple-element.24), channel_id=1, source_target_pairs={{0,1},{1,2},{2,3},{3,4},{4,5},{5,6},{6,7},{8,9},{9,10},{10,11},{11... | collective-permute-start | bytes 331784 | tf_op jit(solution)/shard_map/ppermute | solution.py:217
  85.3 1.3 collective-permute-start.6
  86.6 0.4 collective-permute-done.5
  87.0 5.2 %collective-permute-done.6 = f32[9,24,128]{2,1,0:T(8,128)S(1)} collective-permute-done((f32[9,24,128]{2,1,0:T(8,128)S(1)}, f32[9,24,128]{2,1,0:T(8,128)S(1)}, u32[]{:S(2)}, u32[]{:S(2)}) %collective-permute-start.6) | collective-permute-done | bytes 110624 | tf_op jit(solution)/shard_map/ppermute | solution.py:217
  92.3 0.1 pad_maximum_fusion.15
  92.4 0.4 fusion.17
  92.8 2.3 %collective-permute-start.7 = (f32[9,2,22,128]{3,2,1,0:T(8,128)S(1)}, f32[9,2,22,128]{3,2,1,0:T(8,128)S(1)}, u32[]{:S(2)}, u32[]{:S(2)}) collective-permute-start(f32[9,2,22,128]{3,2,1,0:T(8,128)S(1)} %slice_select_fusion), channel_id=1, source_target_pairs={{0,16},{16,0},{8,24},{24,8},{1,17},{17,1},{9,25},{25,9},{2,18},{18... | collective-permute-start | bytes 608264 | tf_op jit(solution)/shard_map/ppermute | solution.py:236
  95.1 11.5 %collective-permute-start.9 = (f32[9,4,22,128]{3,2,1,0:T(8,128)S(1)}, f32[9,4,22,128]{3,2,1,0:T(8,128)S(1)}, u32[]{:S(2)}, u32[]{:S(2)}) collective-permute-start(f32[9,4,22,128]{3,2,1,0:T(8,128)S(1)} %fusion.17), channel_id=1, source_target_pairs={{8,16},{16,8},{9,17},{17,9},{10,18},{18,10},{11,19},{19,11},{12,20... | collective-permute-start | bytes 1216520 | tf_op jit(solution)/shard_map/ppermute | solution.py:226
  106.5 1.9 collective-permute-start.8
  108.5 4.4 %collective-permute-done.9 = f32[9,4,22,128]{3,2,1,0:T(8,128)S(1)} collective-permute-done((f32[9,4,22,128]{3,2,1,0:T(8,128)S(1)}, f32[9,4,22,128]{3,2,1,0:T(8,128)S(1)}, u32[]{:S(2)}, u32[]{:S(2)}) %collective-permute-start.9) | collective-permute-done | bytes 405536 | tf_op jit(solution)/shard_map/ppermute | solution.py:226
  113.0 0.1 pad_maximum_fusion.1
  113.1 0.6 fusion.2.stack_ref
  113.7 2.6 %shard_map.115 = (f32[192,128]{1,0:T(8,128)S(1)}, f32[2,2048]{1,0:T(2,128)S(1)}) custom-call(f32[2,4,7]{2,1,0:T(4,128)S(1)} %pad_maximum_fusion.18.x_ref, s32[1,2048]{1,0:T(1,128)S(1)} %bitcast.86, s32[1,2048]{1,0:T(1,128)S(1)} %bitcast.90, f32[9,10,22,128]{3,2,1,0:T(8,128)S(1)} %fusion.2.stack_ref, f32[2,7,16,128]{3,2,1,0:T(8,128)S(1)} %broadcast_in_dim.8.y_ref, ...), custom_call_target="tpu_custom_call" | custom-call | tf_op jit(solution)/shard_map/pallas_call | solution.py:326
  116.4 0.4 concatenate.73
  116.7 8.7 %all_to_all.27 = f32[4,108,128]{2,1,0:T(8,128)S(1)} all-to-all(f32[4,108,128]{2,1,0:T(8,128)S(1)} %concatenate.73), channel_id=1, replica_groups={{0,32,64,96},{128,160,192,224},{256,288,320,352},{384,416,448,480},{512..., dimensions={0} | all-to-all | bytes 442368 | tf_op jit(solution)/shard_map/all_to_all | solution.py:206
  125.5 36.0 %psum.15 = f32[108,128]{1,0:T(8,128)S(1)} all-reduce(f32[108,128]{1,0:T(8,128)S(1)} %reduce_sum.19), channel_id=1, replica_groups={{0,128,256,384,512,640,768,896},{32,160,288,416,544,672,800,928},{64,19..., use_global_device_ids=true, to_apply=%region_3.4 | all-reduce | flops 13824 | bytes 110592 | tf_op jit(solution)/shard_map/psum | solution.py:349
  161.4 8.1 %all_to_all.28.total_ref = f32[4,108,128]{2,1,0:T(8,128)S(1)} all-to-all(f32[4,108,128]{2,1,0:T(8,128)S(1)} %broadcast_in_dim.22), channel_id=1, replica_groups={{0,32,64,96},{128,160,192,224},{256,288,320,352},{384,416,448,480},{512..., dimensions={0} | all-to-all | bytes 442368 | tf_op jit(solution)/shard_map/all_to_all | solution.py:206
  169.6 0.7 shard_map.116
  170.3 14.4 %all-to-all-start.3 = ((f32[32,1,128]{2,1,0:T(1,128)}), f32[32,1,128]{2,1,0:T(1,128)S(1)}, u32[]{:S(2)}, u32[]{:S(2)}) async-start(f32[32,1,128]{2,1,0:T(1,128)} %bitcast.40), calls=%async_computation.3 | async-start | bytes 32768 | tf_op jit(solution)/shard_map/all_to_all | solution.py:206
  184.7 6.8 %all-to-all-done.3 = f32[32,1,128]{2,1,0:T(1,128)S(1)} async-done(((f32[32,1,128]{2,1,0:T(1,128)}), f32[32,1,128]{2,1,0:T(1,128)S(1)}, u32[]{:S(2)}, u32[]{:S(2)}) %all-to-all-start.3) | async-done | bytes 16416 | tf_op jit(solution)/shard_map/all_to_all | solution.py:206
  191.5 1.1 shard_map.117
  (46 shorter events, 0.6 us)
Async XLA Ops:
  3.1 14.1 %copy-start.7 = (f32[9,64,128]{2,1,0:T(8,128)S(1)}, f32[9,64,128]{2,1,0:T(8,128)}, u32[]{:S(2)}) copy-start(f32[9,64,128]{2,1,0:T(8,128)} %get-tuple-element.19) | copy-start | bytes 884740
  3.1 9.2 %collective-permute-start = (f32[9,24,128]{2,1,0:T(8,128)}, f32[9,24,128]{2,1,0:T(8,128)S(1)}, u32[]{:S(2)}, u32[]{:S(2)}) collective-permute-start(f32[9,24,128]{2,1,0:T(8,128)} %get-tuple-element.18), channel_id=1, source_target_pairs={{0,1},{1,2},{2,3},{3,4},{4,5},{5,6},{6,7},{8,9},{9,10},{10,11},{11... | collective-permute-start | bytes 331784 | tf_op jit(solution)/shard_map/ppermute | solution.py:217
  8.9 7.2 %collective-permute-start.1 = (f32[9,24,128]{2,1,0:T(8,128)}, f32[9,24,128]{2,1,0:T(8,128)S(1)}, u32[]{:S(2)}, u32[]{:S(2)}) collective-permute-start(f32[9,24,128]{2,1,0:T(8,128)} %get-tuple-element.20), channel_id=1, source_target_pairs={{1,0},{2,1},{3,2},{4,3},{5,4},{6,5},{7,6},{9,8},{10,9},{11,10},{12... | collective-permute-start | bytes 331784 | tf_op jit(solution)/shard_map/ppermute | solution.py:217
  17.2 14.1 %copy-start.1 = (f32[128,128]{1,0:T(8,128)S(1)}, f32[128,128]{1,0:T(8,128)}, u32[]{:S(2)}) copy-start(f32[128,128]{1,0:T(8,128)} %z_ref.1) | copy-start | bytes 196612
  17.6 23.0 %collective-permute-start.4 = (f32[9,4,22,128]{3,2,1,0:T(8,128)S(1)}, f32[9,4,22,128]{3,2,1,0:T(8,128)S(1)}, u32[]{:S(2)}, u32[]{:S(2)}) collective-permute-start(f32[9,4,22,128]{3,2,1,0:T(8,128)S(1)} %fusion.23), channel_id=1, source_target_pairs={{8,16},{16,8},{9,17},{17,9},{10,18},{18,10},{11,19},{19,11},{12,20... | collective-permute-start | bytes 1216520 | tf_op jit(solution)/shard_map/ppermute | solution.py:226
  21.9 18.7 %collective-permute-start.3 = (f32[9,4,22,128]{3,2,1,0:T(8,128)S(1)}, f32[9,4,22,128]{3,2,1,0:T(8,128)S(1)}, u32[]{:S(2)}, u32[]{:S(2)}) collective-permute-start(f32[9,4,22,128]{3,2,1,0:T(8,128)S(1)} %fusion.23), channel_id=1, source_target_pairs={{0,8},{16,24},{8,0},{24,16},{1,9},{17,25},{9,1},{25,17},{2,10},{18... | collective-permute-start | bytes 1216520 | tf_op jit(solution)/shard_map/ppermute | solution.py:227
  31.6 8.9 %collective-permute-start.2 = (f32[9,2,22,128]{3,2,1,0:T(8,128)S(1)}, f32[9,2,22,128]{3,2,1,0:T(8,128)S(1)}, u32[]{:S(2)}, u32[]{:S(2)}) collective-permute-start(f32[9,2,22,128]{3,2,1,0:T(8,128)S(1)} %slice_select_fusion.1), channel_id=1, source_target_pairs={{0,16},{16,0},{8,24},{24,8},{1,17},{17,1},{9,25},{25,9},{2,18},{18... | collective-permute-start | bytes 608264 | tf_op jit(solution)/shard_map/ppermute | solution.py:236
  40.8 1.0 copy-start
  40.8 1.0 copy-start.2
  40.8 1.0 copy-start.3
  40.8 1.0 copy-start.4
  41.4 37.9 %copy-start.5 = (f32[1,1,2048]{2,1,0:T(1,128)S(1)}, f32[1,1,2048]{2,1,0:T(1,128)}, u32[]{:S(2)}) copy-start(f32[1,1,2048]{2,1,0:T(1,128)} %param.15) | copy-start | bytes 24580
  80.0 7.0 %collective-permute-start.5 = (f32[9,24,128]{2,1,0:T(8,128)S(1)}, f32[9,24,128]{2,1,0:T(8,128)S(1)}, u32[]{:S(2)}, u32[]{:S(2)}) collective-permute-start(f32[9,24,128]{2,1,0:T(8,128)S(1)} %get-tuple-element.24), channel_id=1, source_target_pairs={{0,1},{1,2},{2,3},{3,4},{4,5},{5,6},{6,7},{8,9},{9,10},{10,11},{11... | collective-permute-start | bytes 331784 | tf_op jit(solution)/shard_map/ppermute | solution.py:217
  85.3 7.0 %collective-permute-start.6 = (f32[9,24,128]{2,1,0:T(8,128)S(1)}, f32[9,24,128]{2,1,0:T(8,128)S(1)}, u32[]{:S(2)}, u32[]{:S(2)}) collective-permute-start(f32[9,24,128]{2,1,0:T(8,128)S(1)} %get-tuple-element.26), channel_id=1, source_target_pairs={{1,0},{2,1},{3,2},{4,3},{5,4},{6,5},{7,6},{9,8},{10,9},{11,10},{12... | collective-permute-start | bytes 331784 | tf_op jit(solution)/shard_map/ppermute | solution.py:217
  92.8 15.7 %collective-permute-start.7 = (f32[9,2,22,128]{3,2,1,0:T(8,128)S(1)}, f32[9,2,22,128]{3,2,1,0:T(8,128)S(1)}, u32[]{:S(2)}, u32[]{:S(2)}) collective-permute-start(f32[9,2,22,128]{3,2,1,0:T(8,128)S(1)} %slice_select_fusion), channel_id=1, source_target_pairs={{0,16},{16,0},{8,24},{24,8},{1,17},{17,1},{9,25},{25,9},{2,18},{18... | collective-permute-start | bytes 608264 | tf_op jit(solution)/shard_map/ppermute | solution.py:236
  95.1 17.9 %collective-permute-start.9 = (f32[9,4,22,128]{3,2,1,0:T(8,128)S(1)}, f32[9,4,22,128]{3,2,1,0:T(8,128)S(1)}, u32[]{:S(2)}, u32[]{:S(2)}) collective-permute-start(f32[9,4,22,128]{3,2,1,0:T(8,128)S(1)} %fusion.17), channel_id=1, source_target_pairs={{8,16},{16,8},{9,17},{17,9},{10,18},{18,10},{11,19},{19,11},{12,20... | collective-permute-start | bytes 1216520 | tf_op jit(solution)/shard_map/ppermute | solution.py:226
  106.5 6.4 %collective-permute-start.8 = (f32[9,4,22,128]{3,2,1,0:T(8,128)S(1)}, f32[9,4,22,128]{3,2,1,0:T(8,128)S(1)}, u32[]{:S(2)}, u32[]{:S(2)}) collective-permute-start(f32[9,4,22,128]{3,2,1,0:T(8,128)S(1)} %fusion.17), channel_id=1, source_target_pairs={{0,8},{16,24},{8,0},{24,16},{1,9},{17,25},{9,1},{25,17},{2,10},{18... | collective-permute-start | bytes 1216520 | tf_op jit(solution)/shard_map/ppermute | solution.py:227
  116.3 53.2 %copy-start.6 = (f32[1,1,2048]{2,1,0:T(1,128)S(1)}, f32[1,1,2048]{2,1,0:T(1,128)}, u32[]{:S(2)}) copy-start(f32[1,1,2048]{2,1,0:T(1,128)} %param.14) | copy-start | bytes 24580
  170.3 21.2 %all-to-all-start.3 = ((f32[32,1,128]{2,1,0:T(1,128)}), f32[32,1,128]{2,1,0:T(1,128)S(1)}, u32[]{:S(2)}, u32[]{:S(2)}) async-start(f32[32,1,128]{2,1,0:T(1,128)} %bitcast.40), calls=%async_computation.3 | async-start | bytes 32768 | tf_op jit(solution)/shard_map/all_to_all | solution.py:206
